TPU v7x, 32 devices: a whole 2x2x4 slice. The times are simulated.
32 devices in a mesh: dp: 8 (over z, x), mp: 4 (over y, core).
Axes of the slice: x: 2, y: 2, z: 4, core: 2. Of those that a mesh axis runs over, the one named last changes fastest.
Arguments:
- hidden: bfloat16 [10240, 8192], P('dp', 'mp'), may hold values from -6 to 6
- rewards: float32 [64, 160], P('dp'), may hold values from -4 to 4
- lengths: int32 [64], P('dp'), may hold values from 1 to 160, as said below
- dest_shard: int32 [64], P('dp'), may hold values from 0 to 7, as said below
- source_owner: int32 [64], P('dp'), may hold values from 0 to 7, as said below
- pack_offset: int32 [64], P('dp'), may hold values from 0 to 639, as said below
- segment_ids: int32 [5120], P('dp'), may hold values from 0 to 7, as said below
- norm_gain: float32 [8192], replicated, may hold values from 0.5 to 1.5
- w_query: bfloat16 [8192, 4096], P(None, 'mp'), may hold values from -1 to 1
- w_key: bfloat16 [8192, 512], P(None, 'mp'), may hold values from -1 to 1
- w_value: bfloat16 [8192, 512], P(None, 'mp'), may hold values from -0.0625 to 0.0625
- value_head: float32 [8192], P('mp'), may hold values from -0.0625 to 0.0625
- folded_head: float32 [4096], P('mp'), may hold values from -0.09375 to 0.09375
Outputs:
- values: float32 [64, 160], P('dp')
- advantages: float32 [64, 160], P('dp')
Inputs may be any that keep to these rules, and one draw needn't show every extreme that they name: `lengths`: rows of a slot past its rollout's length are unused. Every critic shard holds a rollout of 160 rows. Some owner's 8 rollouts all have 160 rows. `dest_shard`: owner o packs its 8 rollouts on the shards o, o + 1, ..., o + 7, modulo the number of shards, one on each. `source_owner`: shard s packs one rollout from each of the owners s, s - 1, ..., s - 7, modulo the number of shards, in some order, agreeing with dest_shard. `pack_offset`: A shard's packed rollouts lie back to back in the order of their index, each with the length that lengths gives it, and fill all 640 rows. `segment_ids`: each packed row names the index of the packed rollout that holds it, as pack_offset and lengths lay them out.
All inputs are finite; a program needn't handle non-finite values.
Results may differ from a plain program's by a relative error of at most 0.007.
Values may be sent and summed in bfloat16 or wider, within the bound.
No kernel may reach another device: no remote copies, remote signals or barrier semaphores. Data moves between devices by JAX's collectives and lax.ppermute only.
A program may use at most 192 MiB of HBM per device.

v0:
```python
import functools
import math

import jax
import jax.numpy as jnp
from jax import lax
from jax.experimental import pallas as pl
from jax.experimental.pallas import tpu as pltpu
from jax.sharding import PartitionSpec as P

HD = 128
EPSILON = 1e-05
DISCOUNT = 0.99
SMOOTHING = 0.95
ROPE_BASE = 500000.0
DEPTH = 1024
PARTS = 4
GRAIN = 16
ROUTES = (1, 2, 4, 1)
BITS = (1, 2, 4)
SLOT_AT, ARRIVED_AT, SHIP_SLOT, SHIPPED, OVERFLOW = 0, 16, 24, 32, 40


def swapped(value, axis, bit):
    length = lax.axis_size(axis)
    return lax.ppermute(value, axis, [(i, i ^ bit) for i in range(length)])


def lane_groups(value):
    total = value[:, :HD]
    for at in range(HD, value.shape[1], HD):
        total = total + value[:, at : at + HD]
    return total


def add_products(x, gain_ref, wq_ref, wk_ref, wv_ref, q_acc, kv_acc, ss_acc, wkv):
    wkv[:, :HD] = wk_ref[...]
    wkv[:, HD:] = wv_ref[...]
    xf = x.astype(jnp.float32)
    ss_acc[...] += lane_groups(xf * xf)
    scaled = (xf * gain_ref[...]).astype(jnp.bfloat16)
    q_acc[...] += jnp.dot(scaled, wq_ref[...], preferred_element_type=jnp.float32)
    kv_acc[...] += jnp.dot(scaled, wkv[...], preferred_element_type=jnp.float32)


def by_part(step, blocks, x_refs, act):
    for f, refs in enumerate(x_refs):

        @pl.when((step >= f * blocks) & (step < (f + 1) * blocks))
        def _(f=f, refs=refs):
            act(f, refs)


def sums_kernel(parts, groups, begun, part_ref, *refs):
    refs = list(refs)
    take = lambda n: [refs.pop(0) for _ in range(n)]
    x_refs = [take(groups) for _ in range(parts)]
    weights = take(4)
    (head_ref,) = take(1)
    begun_refs = [take(4) for _ in range(groups)] if begun else None
    outs = [take(4) for _ in range(groups)]
    (wkv,) = take(1)
    step = pl.program_id(0)

    @pl.when(step == 0)
    def _():
        for g, out in enumerate(outs):
            for i, ref in enumerate(out):
                ref[...] = begun_refs[g][i][...] if begun else jnp.zeros_like(ref)

    def act(f, rows):
        for x_ref, (q_ref, kv_ref, ss_ref, vt_ref) in zip(rows, outs, strict=True):
            x = x_ref[...]
            if f == 0 and not begun:
                vt_ref[...] += lane_groups(x.astype(jnp.float32) * head_ref[...])
            add_products(x, *weights, q_ref, kv_ref, ss_ref, wkv)

    by_part(step, pl.num_programs(0) // parts, x_refs, act)


def turned(value, cosine, sine):
    return (value * cosine + pltpu.roll(value, HD // 2, 1) * sine).astype(jnp.bfloat16)


def attend_kernel(slot, tile, begin, parts, part_ref, place_ref, *refs):
    x_refs, refs = [[ref] for ref in refs[:parts]], refs[parts:]
    weights, refs = refs[:4], refs[4:]
    (
        q_ref, kv_ref, ss_ref, vt_ref, cos_ref, sin_ref, folded_ref, key_in, val_in,
        out_ref, key_out, val_out, q_acc, kv_acc, ss_acc, cos_rows, sin_rows, place_rows, keys, vals,
        queries, probs, wkv,
    ) = refs
    step = pl.program_id(0)
    steps = pl.num_programs(0)
    rows = q_acc.shape[0]
    heads = q_acc.shape[1] // HD

    @pl.when(step == 0)
    def _():
        q_acc[...] = q_ref[...]
        kv_acc[...] = kv_ref[...]
        ss_acc[...] = ss_ref[...]
        keys[:slot, :] = key_in[...]
        vals[:slot, :HD] = val_in[...]
        vals[:, HD:] = jnp.ones((slot + rows, HD), jnp.bfloat16)
        inner = lax.broadcasted_iota(jnp.int32, (GRAIN, HD), 0)

        def place(b, carry):
            at = place_ref[begin // GRAIN + b]
            here = pl.ds(pl.multiple_of(b * GRAIN, GRAIN), GRAIN)
            there = pl.ds(pl.multiple_of(at * GRAIN, GRAIN), GRAIN)
            cos_rows[here, :] = cos_ref[there, :]
            sin_rows[here, :] = sin_ref[there, :]
            place_rows[here, :] = inner + at * GRAIN
            return carry

        lax.fori_loop(0, rows // GRAIN, place, 0)

    def act(f, rows):
        add_products(rows[0][...], *weights, q_acc, kv_acc, ss_acc, wkv)

    by_part(step, steps // parts, x_refs, act)

    @pl.when(step == steps - 1)
    def _():
        features = DEPTH * steps // parts * PARTS
        scale = lax.rsqrt(jnp.sum(ss_acc[...], axis=1, keepdims=True) / features + EPSILON)
        keys[slot:, :] = turned(kv_acc[:, :HD] * scale, cos_rows[...], sin_rows[...])
        vals[slot:, :HD] = (kv_acc[:, HD:] * scale).astype(jnp.bfloat16)
        key_out[...] = keys[rows:, :]
        val_out[...] = vals[rows:, :HD]
        back = (
            lax.broadcasted_iota(jnp.int32, (tile, slot + tile), 0)
            + slot
            - lax.broadcasted_iota(jnp.int32, (tile, slot + tile), 1)
        )

        def one_tile(t, carry):
            here = pl.ds(pl.multiple_of(t * tile, GRAIN), tile)
            window = pl.ds(pl.multiple_of(t * tile, GRAIN), slot + tile)
            mean = jnp.sum(ss_acc[here, :], axis=1, keepdims=True) / features
            scale = lax.rsqrt(mean + EPSILON) * (math.log2(math.e) / math.sqrt(HD))
            cosine, sine = cos_rows[here, :] * scale, sin_rows[here, :] * scale
            bias = jnp.where((back >= 0) & (back <= place_rows[here, :1]), 0.0, -1e30)
            for h in range(heads):
                turned_h = turned(q_acc[here, h * HD : (h + 1) * HD], cosine, sine)
                queries[h * tile : (h + 1) * tile, :] = turned_h
            scores = lax.dot_general(
                queries[...], keys[window, :], (((1,), (1,)), ((), ())),
                preferred_element_type=jnp.float32,
            )
            for h in range(heads):
                score = scores[h * tile : (h + 1) * tile, :] + bias
                exps = jnp.exp2(score - jnp.max(score, axis=1, keepdims=True))
                probs[h * tile : (h + 1) * tile, :] = exps.astype(jnp.bfloat16)
            attended = jnp.dot(probs[...], vals[window, :], preferred_element_type=jnp.float32)
            total = vt_ref[here, :]
            for h in range(heads):
                mine = attended[h * tile : (h + 1) * tile, :]
                total = total + mine[:, :HD] / mine[:, HD:] * folded_ref[h : h + 1, :]
            out_ref[here, :] = total
            return carry

        lax.fori_loop(0, rows // tile, one_tile, 0, unroll=2)


def start_copy(source, source_block, target, target_block, sem):
    pltpu.make_async_copy(
        source.at[pl.ds(pl.multiple_of(source_block * GRAIN, GRAIN), GRAIN)],
        target.at[pl.ds(pl.multiple_of(target_block * GRAIN, GRAIN), GRAIN)],
        sem,
    ).start()


def wait_copies(source, targets, sems):
    begin = 0
    for target in targets:

        def wait(b, carry, target=target, begin=begin):
            pltpu.make_async_copy(
                source.at[pl.ds(0, GRAIN)],
                target.at[pl.ds(pl.multiple_of(b * GRAIN, GRAIN), GRAIN)],
                sems.at[begin + b],
            ).wait()
            return carry

        lax.fori_loop(0, target.shape[0] // GRAIN, wait, 0)
        begin += target.shape[0] // GRAIN


def blocks_of(length):
    return (length + (GRAIN - 1)) >> (GRAIN.bit_length() - 1)


def lay_out(begin, count, slot_blocks, first_block, source_ref, place_ref):
    def enter(j, carry):
        source_ref[begin + j] = first_block + j
        place_ref[begin + j] = j
        return carry

    lax.fori_loop(0, count, enter, 0)


def lay_out_fill(slot_blocks, source_ref, place_ref):
    def enter(b, carry):
        source_ref[b] = b
        place_ref[b] = lax.rem(b, slot_blocks)
        return carry

    lax.fori_loop(0, source_ref.shape[0], enter, 0)


def first_pack_kernel(slot_blocks, lengths_ref, hidden_ref, place_ref, *refs):
    outs, (source_ref, sems) = refs[:-2], refs[-2:]
    lay_out_fill(slot_blocks, source_ref, place_ref)
    at = jnp.int32(0)
    for i in range(lengths_ref.shape[0]):
        count = blocks_of(lengths_ref[i])
        lay_out(at, count, slot_blocks, i * slot_blocks, source_ref, place_ref)
        at = at + count
    begin = 0
    for out_ref in outs:

        def start(b, carry, out_ref=out_ref, begin=begin):
            start_copy(hidden_ref, source_ref[begin + b], out_ref, b, sems.at[begin + b])
            return carry

        lax.fori_loop(0, out_ref.shape[0] // GRAIN, start, 0)
        begin += out_ref.shape[0] // GRAIN
    wait_copies(hidden_ref, outs, sems)


def plan_kernel(
    slot_blocks, first_blocks, capacity, me_ref, lengths_ref, hidden_ref,
    source_ref, place_ref, info_ref, *refs,
):
    kept, load, sent, moved, sems = refs[len(BITS) :]
    size = slot_blocks * GRAIN
    ships = [
        refs[BITS.index(bit)].at[pl.ds(ROUTES[:r].count(bit) * size, size)]
        for r, bit in enumerate(ROUTES)
    ]
    me = me_ref[0]
    owners = kept.shape[0]
    rollouts = lengths_ref.shape[0] // owners

    def begin(o, carry):
        total = jnp.int32(0)
        for i in range(rollouts):
            total = total + blocks_of(lengths_ref[o * rollouts + i])
        kept[o] = total
        load[o] = jnp.maximum(total, first_blocks)
        sent[o] = 0
        return carry

    lax.fori_loop(0, owners, begin, 0)
    arrived = []
    for r, bit in enumerate(ROUTES):

        def choose(o, carry):
            count = blocks_of(lengths_ref[o * rollouts + rollouts - 1 - sent[o]])
            useful = (kept[o] - count >= first_blocks) & (load[o ^ bit] + count < load[o])
            moved[o] = jnp.where(useful, count, 0)
            return carry

        lax.fori_loop(0, owners, choose, 0)
        slot_now = rollouts - 1 - sent[me]
        info_ref[SHIP_SLOT + r] = slot_now
        info_ref[SHIPPED + r] = jnp.where(moved[me] > 0, 1, 0)
        arrived.append(moved[me ^ bit])
        pltpu.make_async_copy(
            hidden_ref.at[pl.ds(pl.multiple_of(slot_now * size, GRAIN), size)],
            ships[r],
            sems.at[r],
        ).start()

        def move(o, carry):
            kept[o] = kept[o] - moved[o]
            load[o] = load[o] - moved[o] + moved[o ^ bit]
            sent[o] = sent[o] + jnp.where(moved[o] > 0, 1, 0)
            return carry

        lax.fori_loop(0, owners, move, 0)

    most = lax.fori_loop(0, owners, lambda o, m: jnp.maximum(m, load[o]), jnp.int32(0))
    info_ref[OVERFLOW] = jnp.where(most > capacity, 1, 0)

    lay_out_fill(slot_blocks, source_ref, place_ref)
    at = jnp.int32(0)
    for i in range(rollouts):
        here = i < rollouts - sent[me]
        count = jnp.where(here, blocks_of(lengths_ref[me * rollouts + i]), 0)
        info_ref[SLOT_AT + i] = jnp.where(here, at, 0)
        lay_out(at, count, slot_blocks, i * slot_blocks, source_ref, place_ref)
        at = at + count
    at = jnp.maximum(at, first_blocks)
    for r in range(len(ROUTES)):
        info_ref[ARRIVED_AT + r] = jnp.where(arrived[r] > 0, at, 0)
        lay_out(at, arrived[r], slot_blocks, (rollouts + r) * slot_blocks, source_ref, place_ref)
        at = at + arrived[r]
    for r in range(len(ROUTES)):
        pltpu.make_async_copy(hidden_ref.at[pl.ds(0, size)], ships[r], sems.at[r]).wait()


def pack_kernel(begin, slot_blocks, source_ref, hidden_ref, *refs):
    outs, sems = refs[len(BITS) : -1], refs[-1]
    size = slot_blocks * GRAIN
    arrivals = [
        refs[BITS.index(bit)].at[pl.ds(ROUTES[:r].count(bit) * size, size)]
        for r, bit in enumerate(ROUTES)
    ]
    own = hidden_ref.shape[0] // GRAIN
    done = 0
    for out_ref in outs:

        def start(b, carry, out_ref=out_ref, done=done):
            block = source_ref[begin // GRAIN + done + b]

            @pl.when(block < own)
            def _():
                start_copy(hidden_ref, block, out_ref, b, sems.at[done + b])

            for r, arrival in enumerate(arrivals):
                low = own + r * slot_blocks

                @pl.when((block >= low) & (block < low + slot_blocks))
                def _(arrival=arrival, low=low):
                    start_copy(arrival, block - low, out_ref, b, sems.at[done + b])

            return carry

        lax.fori_loop(0, out_ref.shape[0] // GRAIN, start, 0)
        done += out_ref.shape[0] // GRAIN
    wait_copies(hidden_ref, outs, sems)


def unpack_kernel(slot, rollouts, info_ref, *refs):
    totals, out_ref, back_refs, rows_ref = refs[:3], refs[3], refs[4:-1], refs[-1]
    at = 0
    for total in totals:
        rows_ref[at : at + total.shape[0], :] = total[...]
        at += total.shape[0]
    rows_ref[at:, :] = jnp.zeros((rows_ref.shape[0] - at, HD), jnp.float32)
    span = rows_ref.shape[0] - at

    def line(block):
        part = rows_ref[pl.ds(pl.multiple_of(block * GRAIN, GRAIN), span), :]
        return jnp.sum(part.T, axis=0, keepdims=True)[:, :slot]

    for i in range(rollouts):
        out_ref[i : i + 1, :] = line(info_ref[SLOT_AT + i])
    for r, bit in enumerate(ROUTES):
        back_ref, i = back_refs[BITS.index(bit)], ROUTES[:r].count(bit)
        back_ref[i : i + 1, :] = line(info_ref[ARRIVED_AT + r])


def weight_specs(flips, blocks, widths):
    def row(step, part_ref, *rest):
        flip = flips[0]
        for f in range(1, len(flips)):
            flip = jnp.where(step < f * blocks, flip, flips[f])
        return (part_ref[0] ^ flip) * blocks + lax.rem(step, blocks)

    return [pl.BlockSpec((1, DEPTH), lambda k, *p: (0, row(k, *p)))] + [
        pl.BlockSpec((DEPTH, width), lambda k, *p: (row(k, *p), 0)) for width in widths
    ]


def x_spec(rows, blocks, f):
    return pl.BlockSpec((rows, DEPTH), lambda k, *p: (0, jnp.clip(k - f * blocks, 0, blocks - 1)))


def fixed(*shape):
    return pl.BlockSpec(shape, lambda k, *p: (0, 0))


def cost(rows, depth, columns):
    return pl.CostEstimate(
        flops=2 * rows * depth * columns,
        bytes_accessed=2 * depth * (rows + columns) + 4 * rows * columns,
        transcendentals=0,
    )


def sums_call(shared, flips, xs, head, begun=None):
    part, gain, weights = shared
    widths = [w.shape[1] for w in weights]
    groups = len(xs[0])
    blocks = xs[0][0].shape[1] // DEPTH
    counts = [x.shape[0] for x in xs[0]]
    outs = [(count, width) for count in counts for width in (widths[0], sum(widths[1:]), HD, HD)]
    given = [a for group in begun for a in group] if begun else []
    sums = pl.pallas_call(
        functools.partial(sums_kernel, len(flips), groups, begun is not None),
        grid_spec=pltpu.PrefetchScalarGridSpec(
            num_scalar_prefetch=1,
            grid=(len(flips) * blocks,),
            in_specs=[x_spec(count, blocks, f) for f in range(len(flips)) for count in counts]
            + weight_specs(flips, blocks, widths)
            + [pl.BlockSpec((1, DEPTH), lambda k, *p: (0, jnp.minimum(k, blocks - 1)))]
            + [fixed(*a.shape) for a in given],
            out_specs=[fixed(*shape) for shape in outs],
            scratch_shapes=[pltpu.VMEM((DEPTH, 2 * HD), jnp.bfloat16)],
        ),
        out_shape=[jax.ShapeDtypeStruct(shape, jnp.float32) for shape in outs],
        compiler_params=pltpu.CompilerParams(vmem_limit_bytes=24 << 20),
        cost_estimate=cost(sum(counts), len(flips) * blocks * DEPTH, sum(widths)),
        name="sums",
    )(part, *[x for row in xs for x in row], gain, *weights, head, *given)
    return [sums[4 * g : 4 * g + 4] for g in range(groups)]


def attend_call(shared, tables, begin, places, flips, xs, sums, before):
    part, gain, weights = shared
    widths = [w.shape[1] for w in weights]
    count, blocks = xs[0].shape[0], xs[0].shape[1] // DEPTH
    slot = tables[0].shape[0]
    tile = max(t for t in range(GRAIN, slot // 2 + 1, GRAIN) if count % t == 0)
    stacked = widths[0] // HD * tile
    return pl.pallas_call(
        functools.partial(attend_kernel, slot, tile, begin, len(flips)),
        grid_spec=pltpu.PrefetchScalarGridSpec(
            num_scalar_prefetch=2,
            grid=(len(flips) * blocks,),
            in_specs=[x_spec(count, blocks, f) for f in range(len(flips))]
            + weight_specs(flips, blocks, widths)
            + [fixed(*a.shape) for a in (*sums, *tables, *before)],
            out_specs=[fixed(count, HD), fixed(slot, HD), fixed(slot, HD)],
            scratch_shapes=[
                pltpu.VMEM((count, widths[0]), jnp.float32),
                pltpu.VMEM((count, widths[1] + widths[2]), jnp.float32),
                pltpu.VMEM((count, HD), jnp.float32),
                pltpu.VMEM((count, HD), jnp.float32),
                pltpu.VMEM((count, HD), jnp.float32),
                pltpu.VMEM((count, HD), jnp.int32),
                pltpu.VMEM((slot + count, HD), jnp.bfloat16),
                pltpu.VMEM((slot + count, 2 * HD), jnp.bfloat16),
                pltpu.VMEM((stacked, HD), jnp.bfloat16),
                pltpu.VMEM((stacked, slot + tile), jnp.bfloat16),
                pltpu.VMEM((DEPTH, 2 * HD), jnp.bfloat16),
            ],
        ),
        out_shape=[
            jax.ShapeDtypeStruct((count, HD), jnp.float32),
            jax.ShapeDtypeStruct((slot, HD), jnp.bfloat16),
            jax.ShapeDtypeStruct((slot, HD), jnp.bfloat16),
        ],
        compiler_params=pltpu.CompilerParams(vmem_limit_bytes=24 << 20),
        cost_estimate=cost(count, len(flips) * blocks * DEPTH, sum(widths)),
        name="attend",
    )(part, places, *xs, gain, *weights, *sums, *tables, *before)


def local(
    hidden,
    rewards,
    lengths,
    dest_shard,
    source_owner,
    pack_offset,
    segment_ids,
    norm_gain,
    w_query,
    w_key,
    w_value,
    value_head,
    folded_head,
):
    rollouts, slot = rewards.shape
    rows, part_width = hidden.shape
    q_width = w_query.shape[1]
    part = lax.axis_index("mp").astype(jnp.int32)[None]
    gain = norm_gain[None, :]
    weights = (w_query, w_key, w_value)

    positions = jnp.arange(slot, dtype=jnp.float32)
    half = HD // 2
    frequency = ROPE_BASE ** (-jnp.arange(half, dtype=jnp.float32) / half)
    angles = positions[:, None] * frequency[None, :]
    cosine = jnp.concatenate([jnp.cos(angles)] * 2, axis=1)
    sine = jnp.concatenate([-jnp.sin(angles), jnp.sin(angles)], axis=1)

    slot_blocks = slot // GRAIN
    packed = segment_ids.shape[0]
    first = packed * 4 // 5
    second = packed * 3 // 5
    rest = rows - first - second
    whole = jax.ShapeDtypeStruct
    anywhere = pl.BlockSpec(memory_space=pl.ANY)
    scalars = pl.BlockSpec(memory_space=pltpu.SMEM)
    onchip = pl.BlockSpec(memory_space=pltpu.VMEM)
    blocks_in_all = rows // GRAIN
    shared = (part, gain, weights)
    head = value_head[None, :]
    tables = (cosine, sine, folded_head.reshape(q_width // HD, HD))
    vmem = pltpu.CompilerParams(vmem_limit_bytes=12 << 20)

    places_first, x_first = pl.pallas_call(
        functools.partial(first_pack_kernel, slot_blocks),
        in_specs=[scalars, anywhere],
        out_specs=[scalars, onchip],
        out_shape=[whole((blocks_in_all,), jnp.int32), whole((first, part_width), hidden.dtype)],
        scratch_shapes=[
            pltpu.SMEM((blocks_in_all,), jnp.int32),
            pltpu.SemaphoreType.DMA((first // GRAIN,)),
        ],
        compiler_params=vmem,
        name="first_pack",
    )(lengths, hidden)
    far_first = swapped(x_first, "mp", 2)
    near_first = swapped(x_first, "mp", 1)

    owners = lax.axis_size("dp")
    me = lax.axis_index("dp").astype(jnp.int32)
    everyone = lax.psum(
        jnp.where(jnp.arange(owners)[:, None] == me, lengths[None, :], 0), "dp"
    ).reshape(-1)
    source, places, info, *ships = pl.pallas_call(
        functools.partial(
            plan_kernel, slot_blocks, first // GRAIN, (first + second) // GRAIN
        ),
        in_specs=[scalars, scalars, anywhere],
        out_specs=[scalars, scalars, scalars] + [onchip] * len(BITS),
        out_shape=[
            whole((blocks_in_all,), jnp.int32),
            whole((blocks_in_all,), jnp.int32),
            whole((64,), jnp.int32),
        ]
        + [whole((ROUTES.count(bit) * slot, part_width), hidden.dtype) for bit in BITS],
        scratch_shapes=[pltpu.SMEM((owners,), jnp.int32)] * 4
        + [pltpu.SemaphoreType.DMA((len(ROUTES),))],
        compiler_params=vmem,
        name="plan",
    )(me[None], everyone, hidden)
    arrivals = [swapped(ship, "dp", bit) for ship, bit in zip(ships, BITS, strict=True)]

    shipped = info[SHIPPED : SHIPPED + len(ROUTES)] > 0
    ship_slots = info[SHIP_SLOT : SHIP_SLOT + len(ROUTES)]
    mine = shipped[:, None] & (ship_slots[:, None] == jnp.arange(rollouts)[None, :])

    def pack(begin, count):
        return pl.pallas_call(
            functools.partial(pack_kernel, begin, slot_blocks),
            in_specs=[scalars, anywhere] + [anywhere] * len(BITS),
            out_specs=onchip,
            out_shape=whole((count, part_width), hidden.dtype),
            scratch_shapes=[pltpu.SemaphoreType.DMA((count // GRAIN,))],
            compiler_params=vmem,
            name="pack",
        )(source, hidden, *arrivals)

    def attend(begin, places, far, sums, before):
        return attend_call(
            shared, tables, begin, places, (2, 3), [far, swapped(far, "mp", 1)], sums, before
        )

    nothing = jnp.zeros((slot, HD), jnp.bfloat16)
    before = (nothing, nothing)
    (sums_first,) = sums_call(shared, (0, 1), [[x_first], [near_first]], head)
    far_first, mine, sums_first, *arrivals = lax.optimization_barrier(
        (far_first, mine, sums_first, *arrivals)
    )
    x_second = pack(first, second)
    far_second = swapped(x_second, "mp", 2)
    near_second = swapped(x_second, "mp", 1)
    total_first, *before = attend(0, places_first, far_first, sums_first, before)
    x_second, near_second, _ = lax.optimization_barrier((x_second, near_second, total_first))
    (sums_second,) = sums_call(shared, (0, 1), [[x_second], [near_second]], head)
    far_second, sums_second = lax.optimization_barrier((far_second, sums_second))
    far_near = swapped(far_second, "mp", 1)
    (sums_second,) = sums_call(shared, (2,), [[far_second]], head, begun=[sums_second])
    far_near, sums_second = lax.optimization_barrier((far_near, sums_second))
    total_second, *before = attend_call(
        shared, tables, first, places, (3,), [far_near], sums_second, before
    )

    def overflow(before):
        begin = first + second
        x = pack(begin, rest)
        (sums,) = sums_call(shared, (0, 1), [[x], [swapped(x, "mp", 1)]], head)
        return attend(begin, places, swapped(x, "mp", 2), sums, before)[0]

    total_rest = lax.cond(
        info[OVERFLOW] > 0, overflow, lambda _: jnp.zeros((rest, HD), jnp.float32), before
    )
    totals = (total_first, total_second, total_rest)
    slot_terms, *backs = pl.pallas_call(
        functools.partial(unpack_kernel, slot, rollouts),
        in_specs=[scalars] + [onchip] * len(totals),
        out_shape=[whole((rollouts, slot), jnp.float32)]
        + [whole((ROUTES.count(bit), slot), jnp.float32) for bit in BITS],
        scratch_shapes=[pltpu.VMEM((rows + 2 * HD, HD), jnp.float32)],
        name="unpack",
    )(info, *totals)
    backs = [swapped(back, "dp", bit) for back, bit in zip(backs, BITS, strict=True)]
    for r, bit in enumerate(ROUTES):
        back = backs[BITS.index(bit)][ROUTES[:r].count(bit)]
        slot_terms = jnp.where(mine[r, :, None], back[None, :], slot_terms)
    slot_values = slot_terms
    for bit in (1, 2):
        slot_values = slot_values + swapped(slot_values, "mp", bit)

    step_ids = jnp.arange(slot, dtype=jnp.int32)
    live_mask = step_ids[None, :] < lengths[:, None]
    values = jnp.where(live_mask, slot_values, 0.0)
    next_live = step_ids[None, :] + 1 < lengths[:, None]
    following = jnp.concatenate([values[:, 1:], jnp.zeros((rollouts, 1), jnp.float32)], axis=1)
    one_step = jnp.where(
        live_mask, rewards + DISCOUNT * jnp.where(next_live, following, 0.0) - values, 0.0
    )
    lag_matrix = (step_ids[:, None] - step_ids[None, :]).astype(jnp.float32)
    decay_table = jnp.where(
        lag_matrix >= 0, jnp.exp(lag_matrix * math.log(DISCOUNT * SMOOTHING)), 0.0
    )
    advantages = jnp.dot(one_step, decay_table, precision=lax.Precision.HIGHEST)
    return (values, advantages)


def solution(mesh):
    return jax.shard_map(
        local,
        mesh=mesh,
        in_specs=(
            P("dp", "mp"),
            P("dp", None),
            P("dp"),
            P("dp"),
            P("dp"),
            P("dp"),
            P("dp"),
            P(),
            P(None, "mp"),
            P(None, "mp"),
            P(None, "mp"),
            P("mp"),
            P("mp"),
        ),
        out_specs=(P("dp", None), P("dp", None)),
        check_vma=False,
    )
```

profile of v0, /device:TPU:0, one launch (start us, length us, event | category | flops | bytes accessed | tf_op | source)
XLA Modules:
  0.0 124.4 jit_solution(3107258778019341841)
XLA Ops:
  0.6 0.6 copy-done.2
  1.3 4.0 %first_pack.1 = (s32[80]{0:T(128)S(1)}, bf16[512,2048]{1,0:T(8,128)(2,1)S(1)}) custom-call(s32[8]{0:T(128)S(1)} %copy-done.2, bf16[1280,2048]{1,0:T(8,128)(2,1)} %hidden_ref.5), custom_call_target="tpu_custom_call" | custom-call | tf_op jit(solution)/shard_map/first_pack/pallas_call | solution.py:498
  5.3 0.5 collective-permute-start.4
  5.8 2.6 %collective-permute-start.3 = (bf16[512,2048]{1,0:T(8,128)(2,1)S(1)}, bf16[512,2048]{1,0:T(8,128)(2,1)}, u32[]{:S(2)}, u32[]{:S(2)}) collective-permute-start(bf16[512,2048]{1,0:T(8,128)(2,1)S(1)} %get-tuple-element.112.refs_0_), channel_id=1, source_target_pairs={{0,2},{1,3},{2,0},{3,1},{4,6},{5,7},{6,4},{7,5},{8,10},{9,11},{10,... | collective-permute-start | bytes 6291464 | tf_op jit(solution)/shard_map/ppermute | solution.py:26
  8.4 0.1 broadcast_select_fusion
  8.5 0.1 reshape.38
  8.5 11.6 %psum.7.lengths_ref = s32[64]{0:T(128)S(1)} all-reduce(s32[64]{0:T(128)S(1)} %reshape.38), channel_id=1, replica_groups=mesh['dp'=8,'mp'=4] {'dp'}, use_global_device_ids=true, to_apply=%region_0.1 | all-reduce | flops 64 | bytes 512 | tf_op jit(solution)/shard_map/psum | solution.py:515
  20.2 3.8 %plan.1 = (s32[80]{0:T(128)S(1)}, s32[80]{0:T(128)S(1)}, s32[64]{0:T(128)S(1)}, bf16[320,2048]{1,0:T(8,128)(2,1)S(1)}, bf16[160,2048]{1,0:T(8,128)(2,1)}, /*index=5*/bf16[160,2048]{1,0:T(8,128)(2,1)}) custom-call(s32[1]{0:T(128)} %bitcast.me_ref, s32[64]{0:T(128)S(1)} %psum.7.lengths_ref, bf16[1280,2048]{1,0:T(8,128)(2,1)} %hidden_ref.5), custom_call_target="tpu_custom_call" | custom-call | tf_op jit(solution)/shard_map/plan/pallas_call | solution.py:518
  24.0 1.5 %collective-permute-start.5 = (bf16[320,2048]{1,0:T(8,128)(2,1)S(1)}, bf16[320,2048]{1,0:T(8,128)(2,1)}, u32[]{:S(2)}, u32[]{:S(2)}) collective-permute-start(bf16[320,2048]{1,0:T(8,128)(2,1)S(1)} %get-tuple-element.118), channel_id=1, source_target_pairs={{0,4},{4,0},{8,12},{12,8},{16,20},{20,16},{24,28},{28,24},{1,5},{5... | collective-permute-start | bytes 3932168 | tf_op jit(solution)/shard_map/ppermute | solution.py:26
  25.5 0.4 collective-permute-start.6
  25.9 0.5 collective-permute-start.7
  26.4 0.1 slice.31
  26.5 0.1 slice_compare_fusion
  26.6 0.1 fusion.24
  26.7 0.0 slice-start
  26.7 11.0 %sums.5 = (f32[512,1024]{1,0:T(8,128)S(1)}, f32[512,256]{1,0:T(8,128)S(1)}, f32[512,128]{1,0:T(8,128)S(1)}, f32[512,128]{1,0:T(8,128)S(1)}) custom-call(s32[1]{0:T(128)} %bitcast.1.part_ref, bf16[512,2048]{1,0:T(8,128)(2,1)S(1)} %get-tuple-element.112.refs_0_, bf16[512,2048]{1,0:T(8,128)(2,1)} %collective-permute-done.4.refs_1_, f32[1,8192]{1,0:T(1,128)S(1)} %bitcast.22, ...), custom_call_target="tpu_custom_call" | custom-call | flops 5368709120 | bytes 17301504 | tf_op jit(solution)/shard_map/sums/pallas_call | solution.py:393
  37.7 15.4 %collective-permute-done.6.refs_1_ = bf16[160,2048]{1,0:T(8,128)(2,1)} collective-permute-done((bf16[160,2048]{1,0:T(8,128)(2,1)}, bf16[160,2048]{1,0:T(8,128)(2,1)}, u32[]{:S(2)}, u32[]{:S(2)}) %collective-permute-start.6) | collective-permute-done | bytes 655392 | tf_op jit(solution)/shard_map/ppermute | solution.py:26
  53.1 2.3 %collective-permute-done.7.refs_2_ = bf16[160,2048]{1,0:T(8,128)(2,1)} collective-permute-done((bf16[160,2048]{1,0:T(8,128)(2,1)}, bf16[160,2048]{1,0:T(8,128)(2,1)}, u32[]{:S(2)}, u32[]{:S(2)}) %collective-permute-start.7) | collective-permute-done | bytes 655392 | tf_op jit(solution)/shard_map/ppermute | solution.py:26
  55.4 0.0 slice-start.3
  55.4 0.0 copy-start.5
  55.4 0.0 copy-start.6
  55.4 0.0 copy-start.9
  55.5 3.6 %pack.3.refs_0_ = bf16[384,2048]{1,0:T(8,128)(2,1)S(1)} custom-call(s32[80]{0:T(128)S(1)} %get-tuple-element.130.source_ref, bf16[1280,2048]{1,0:T(8,128)(2,1)S(1)} %bitcast.21, bf16[320,2048]{1,0:T(8,128)(2,1)} %collective-permute-done.5.refs_0_, bf16[160,2048]{1,0:T(8,128)(2,1)} %collective-permute-done.6.refs_1_, ...), custom_call_target="tpu_custom_call" | custom-call | tf_op jit(solution)/shard_map/pack/pallas_call | solution.py:542
  59.1 0.5 collective-permute-start.10
  59.6 1.1 collective-permute-start.9
  60.7 0.3 fusion.12
  61.1 0.1 pad_maximum_fusion
  61.3 13.8 %attend.4 = (f32[512,128]{1,0:T(8,128)S(1)}, bf16[160,128]{1,0:T(8,128)(2,1)S(1)}, bf16[160,128]{1,0:T(8,128)(2,1)S(1)}) custom-call(s32[1]{0:T(128)} %bitcast.1.part_ref, s32[80]{0:T(128)S(1)} %get-tuple-element.122.place_ref, bf16[512,2048]{1,0:T(8,128)(2,1)} %collective-permute-done.3.refs_0_, bf16[512,2048]{1,0:T(8,128)(2,1)S(1)} %collective-permute-done.8.refs_1_, ...), custom_call_target="tpu_custom_call" | custom-call | flops 5368709120 | bytes 17301504 | tf_op jit(solution)/shard_map/attend/pallas_call | solution.py:420
  75.1 6.1 %sums.6 = (f32[384,1024]{1,0:T(8,128)S(1)}, f32[384,256]{1,0:T(8,128)S(1)}, f32[384,128]{1,0:T(8,128)S(1)}, f32[384,128]{1,0:T(8,128)S(1)}) custom-call(s32[1]{0:T(128)} %bitcast.1.part_ref, bf16[384,2048]{1,0:T(8,128)(2,1)S(1)} %pack.3.refs_0_, bf16[384,2048]{1,0:T(8,128)(2,1)S(1)} %collective-permute-done.10.refs_1_, f32[1,8192]{1,0:T(1,128)S(1)} %bitcast.24, ...), custom_call_target="tpu_custom_call" | custom-call | flops 4026531840 | bytes 15597568 | tf_op jit(solution)/shard_map/sums/pallas_call | solution.py:393
  81.2 14.8 %collective-permute-done.9.refs_0_ = bf16[384,2048]{1,0:T(8,128)(2,1)S(1)} collective-permute-done((bf16[384,2048]{1,0:T(8,128)(2,1)S(1)}, bf16[384,2048]{1,0:T(8,128)(2,1)S(1)}, u32[]{:S(2)}, u32[]{:S(2)}) %collective-permute-start.9) | collective-permute-done | bytes 1572896 | tf_op jit(solution)/shard_map/ppermute | solution.py:26
  96.0 0.6 slice.33
  97.3 3.0 %sums.7 = (f32[384,1024]{1,0:T(8,128)S(1)}, f32[384,256]{1,0:T(8,128)S(1)}, f32[384,128]{1,0:T(8,128)S(1)}, f32[384,128]{1,0:T(8,128)S(1)}) custom-call(s32[1]{0:T(128)} %bitcast.1.part_ref, bf16[384,2048]{1,0:T(8,128)(2,1)S(1)} %collective-permute-done.9.refs_0_, f32[1,8192]{1,0:T(1,128)S(1)} %bitcast.25, bf16[8192,1024]{1,0:T(8,128)(2,1)S(1)} %bitcast.19, ...), custom_call_target="tpu_custom_call" | custom-call | flops 2013265920 | bytes 8781824 | tf_op jit(solution)/shard_map/sums/pallas_call | solution.py:393
  100.2 7.3 %attend.5 = (f32[384,128]{1,0:T(8,128)S(1)}, bf16[160,128]{1,0:T(8,128)(2,1)S(1)}, bf16[160,128]{1,0:T(8,128)(2,1)S(1)}) custom-call(s32[1]{0:T(128)} %bitcast.1.part_ref, s32[80]{0:T(128)S(1)} %get-tuple-element.129.place_ref, bf16[384,2048]{1,0:T(8,128)(2,1)S(1)} %collective-permute-done.11.refs_0_, f32[1,8192]{1,0:T(1,128)S(1)} %bitcast.26, ...), custom_call_target="tpu_custom_call" | custom-call | flops 2013265920 | bytes 8781824 | tf_op jit(solution)/shard_map/attend/pallas_call | solution.py:420
  107.5 0.7 copy-done.1
  108.2 2.1 %unpack.1 = (f32[8,160]{1,0:T(8,128)}, f32[2,160]{1,0:T(2,128)}, f32[1,160]{1,0:T(1,128)}, f32[1,160]{1,0:T(1,128)}) custom-call(s32[64]{0:T(128)} %copy-done.4, f32[512,128]{1,0:T(8,128)} %copy-done, f32[384,128]{1,0:T(8,128)} %copy-done.1, f32[384,128]{1,0:T(8,128)S(1)} %get-tuple-element.174.refs_2_), custom_call_target="tpu_custom_call" | custom-call | tf_op jit(solution)/shard_map/unpack/pallas_call | solution.py:587
  110.4 0.9 collective-permute-start.12
  111.2 0.8 collective-permute-start.14
  112.0 3.3 %collective-permute-start.13 = (f32[1,160]{1,0:T(1,128)}, f32[1,160]{1,0:T(1,128)S(1)}, u32[]{:S(2)}, u32[]{:S(2)}) collective-permute-start(f32[1,160]{1,0:T(1,128)} %get-tuple-element.160), channel_id=1, source_target_pairs={{0,16},{4,20},{8,24},{12,28},{16,0},{20,4},{24,8},{28,12},{1,17},{... | collective-permute-start | bytes 1928 | tf_op jit(solution)/shard_map/ppermute | solution.py:26
  115.3 1.7 %collective-permute-done.13 = f32[1,160]{1,0:T(1,128)S(1)} collective-permute-done((f32[1,160]{1,0:T(1,128)}, f32[1,160]{1,0:T(1,128)S(1)}, u32[]{:S(2)}, u32[]{:S(2)}) %collective-permute-start.13) | collective-permute-done | bytes 672 | tf_op jit(solution)/shard_map/ppermute | solution.py:26
  117.0 0.8 select_select_fusion
  117.8 0.0 collective-permute-start.15
  117.8 1.2 collective-permute-done.15
  119.0 0.8 fusion.29
  119.7 1.5 %collective-permute-start.16 = (f32[8,160]{1,0:T(8,128)S(1)}, f32[8,160]{1,0:T(8,128)S(1)}, u32[]{:S(2)}, u32[]{:S(2)}) collective-permute-start(f32[8,160]{1,0:T(8,128)S(1)} %fusion.29), channel_id=1, source_target_pairs={{0,2},{1,3},{2,0},{3,1},{4,6},{5,7},{6,4},{7,5},{8,10},{9,11},{10,... | collective-permute-start | bytes 15368 | tf_op jit(solution)/shard_map/ppermute | solution.py:26
  121.3 2.1 %collective-permute-done.16 = f32[8,160]{1,0:T(8,128)S(1)} collective-permute-done((f32[8,160]{1,0:T(8,128)S(1)}, f32[8,160]{1,0:T(8,128)S(1)}, u32[]{:S(2)}, u32[]{:S(2)}) %collective-permute-start.16) | collective-permute-done | bytes 5152 | tf_op jit(solution)/shard_map/ppermute | solution.py:26
  123.4 0.1 add_select_fusion
  123.5 0.1 slice.42
  123.6 0.8 fusion
  (49 shorter events, 0.2 us)
Async XLA Ops:
  0.6 0.7 copy-start.2
  1.3 7.1 %copy-start.3 = (s32[8]{0:T(128)S(1)}, s32[8]{0:T(128)}, u32[]{:S(2)}) copy-start(s32[8]{0:T(128)} %lengths_ref.1) | copy-start | bytes 100
  5.3 21.4 %collective-permute-start.4 = (bf16[512,2048]{1,0:T(8,128)(2,1)S(1)}, bf16[512,2048]{1,0:T(8,128)(2,1)}, u32[]{:S(2)}, u32[]{:S(2)}) collective-permute-start(bf16[512,2048]{1,0:T(8,128)(2,1)S(1)} %get-tuple-element.112.refs_0_), channel_id=1, source_target_pairs={{0,1},{1,0},{2,3},{3,2},{4,5},{5,4},{6,7},{7,6},{8,9},{9,8},{10,11... | collective-permute-start | bytes 6291464 | tf_op jit(solution)/shard_map/ppermute | solution.py:26
  5.8 49.6 %collective-permute-start.3 = (bf16[512,2048]{1,0:T(8,128)(2,1)S(1)}, bf16[512,2048]{1,0:T(8,128)(2,1)}, u32[]{:S(2)}, u32[]{:S(2)}) collective-permute-start(bf16[512,2048]{1,0:T(8,128)(2,1)S(1)} %get-tuple-element.112.refs_0_), channel_id=1, source_target_pairs={{0,2},{1,3},{2,0},{3,1},{4,6},{5,7},{6,4},{7,5},{8,10},{9,11},{10,... | collective-permute-start | bytes 6291464 | tf_op jit(solution)/shard_map/ppermute | solution.py:26
  20.2 6.5 %copy-start.7 = (f32[8192]{0:T(1024)S(1)}, f32[8192]{0:T(1024)}, u32[]{:S(2)}) copy-start(f32[8192]{0:T(1024)} %param.18) | copy-start | bytes 98308
  20.2 6.5 %copy-start.8 = (f32[2048]{0:T(1024)S(1)}, f32[2048]{0:T(1024)}, u32[]{:S(2)}) copy-start(f32[2048]{0:T(1024)} %param.22) | copy-start | bytes 24580
  24.0 72.1 %copy-start.4 = (s32[64]{0:T(128)}, s32[64]{0:T(128)S(1)}, u32[]{:S(2)}) copy-start(s32[64]{0:T(128)S(1)} %get-tuple-element.113.info_ref) | copy-start | bytes 772
  24.0 31.4 %collective-permute-start.5 = (bf16[320,2048]{1,0:T(8,128)(2,1)S(1)}, bf16[320,2048]{1,0:T(8,128)(2,1)}, u32[]{:S(2)}, u32[]{:S(2)}) collective-permute-start(bf16[320,2048]{1,0:T(8,128)(2,1)S(1)} %get-tuple-element.118), channel_id=1, source_target_pairs={{0,4},{4,0},{8,12},{12,8},{16,20},{20,16},{24,28},{28,24},{1,5},{5... | collective-permute-start | bytes 3932168 | tf_op jit(solution)/shard_map/ppermute | solution.py:26
  25.5 27.6 %collective-permute-start.6 = (bf16[160,2048]{1,0:T(8,128)(2,1)}, bf16[160,2048]{1,0:T(8,128)(2,1)}, u32[]{:S(2)}, u32[]{:S(2)}) collective-permute-start(bf16[160,2048]{1,0:T(8,128)(2,1)} %get-tuple-element.119), channel_id=1, source_target_pairs={{0,8},{4,12},{8,0},{12,4},{16,24},{20,28},{24,16},{28,20},{1,9},{5... | collective-permute-start | bytes 1966088 | tf_op jit(solution)/shard_map/ppermute | solution.py:26
  25.9 29.5 %collective-permute-start.7 = (bf16[160,2048]{1,0:T(8,128)(2,1)}, bf16[160,2048]{1,0:T(8,128)(2,1)}, u32[]{:S(2)}, u32[]{:S(2)}) collective-permute-start(bf16[160,2048]{1,0:T(8,128)(2,1)} %get-tuple-element.120), channel_id=1, source_target_pairs={{0,16},{4,20},{8,24},{12,28},{16,0},{20,4},{24,8},{28,12},{1,17},{... | collective-permute-start | bytes 1966088 | tf_op jit(solution)/shard_map/ppermute | solution.py:26
  26.6 28.7 %slice-start.4 = ((s8[5242880]{0:T(1024)(128)(4,1)}), s8[4194304]{0:T(1024)(128)(4,1)S(1)}, s32[]{:S(2)}) async-start(s8[5242880]{0:T(1024)(128)(4,1)} %bitcast.20), calls=%async_computation.4 | async-start | bytes 8388608
  26.6 28.7 %slice-start.5 = ((s8[5242880]{0:T(1024)(128)(4,1)}), s8[1048576]{0:T(1024)(128)(4,1)S(1)}, s32[]{:S(2)}) async-start(s8[5242880]{0:T(1024)(128)(4,1)} %bitcast.20), calls=%async_computation.5 | async-start | bytes 2097152
  26.7 34.6 %slice-start = ((s8[16777216]{0:T(1024)(128)(4,1)}), s8[4194304]{0:T(1024)(128)(4,1)S(1)}, s32[]{:S(2)}) async-start(s8[16777216]{0:T(1024)(128)(4,1)} %bitcast.18), calls=%async_computation | async-start | bytes 8388608
  26.7 34.6 %slice-start.1 = ((s8[16777216]{0:T(1024)(128)(4,1)}), s8[4194304]{0:T(1024)(128)(4,1)S(1)}, s32[]{:S(2)}) async-start(s8[16777216]{0:T(1024)(128)(4,1)} %bitcast.18), calls=%async_computation.1 | async-start | bytes 8388608
  26.7 34.6 %slice-start.2 = ((s8[16777216]{0:T(1024)(128)(4,1)}), s8[4194304]{0:T(1024)(128)(4,1)S(1)}, s32[]{:S(2)}) async-start(s8[16777216]{0:T(1024)(128)(4,1)} %bitcast.18), calls=%async_computation.2 | async-start | bytes 8388608
  55.4 5.8 %collective-permute-start.8 = (bf16[512,2048]{1,0:T(8,128)(2,1)}, bf16[512,2048]{1,0:T(8,128)(2,1)S(1)}, u32[]{:S(2)}, u32[]{:S(2)}) collective-permute-start(bf16[512,2048]{1,0:T(8,128)(2,1)} %collective-permute-done.3.refs_0_), channel_id=1, source_target_pairs={{0,1},{1,0},{2,3},{3,2},{4,5},{5,4},{6,7},{7,6},{8,9},{9,8},{10,11... | collective-permute-start | bytes 6291464 | tf_op jit(solution)/shard_map/ppermute | solution.py:26
  55.4 5.8 %slice-start.3 = ((s8[16777216]{0:T(1024)(128)(4,1)}), s8[4194304]{0:T(1024)(128)(4,1)S(1)}, s32[]{:S(2)}) async-start(s8[16777216]{0:T(1024)(128)(4,1)} %bitcast.18), calls=%async_computation.3 | async-start | bytes 8388608
  55.4 5.8 %copy-start.5 = (bf16[8192,128]{1,0:T(8,128)(2,1)S(1)}, bf16[8192,128]{1,0:T(8,128)(2,1)}, u32[]{:S(2)}) copy-start(bf16[8192,128]{1,0:T(8,128)(2,1)} %refs_3_.9) | copy-start | bytes 6291460
  55.4 5.8 %copy-start.6 = (bf16[8192,128]{1,0:T(8,128)(2,1)S(1)}, bf16[8192,128]{1,0:T(8,128)(2,1)}, u32[]{:S(2)}) copy-start(bf16[8192,128]{1,0:T(8,128)(2,1)} %refs_4_.9) | copy-start | bytes 6291460
  55.4 5.8 %copy-start.9 = (f32[1024]{0:T(1024)S(1)}, f32[1024]{0:T(1024)}, u32[]{:S(2)}) copy-start(f32[1024]{0:T(1024)} %param.23) | copy-start | bytes 12292
  59.1 16.0 %collective-permute-start.10 = (bf16[384,2048]{1,0:T(8,128)(2,1)S(1)}, bf16[384,2048]{1,0:T(8,128)(2,1)S(1)}, u32[]{:S(2)}, u32[]{:S(2)}) collective-permute-start(bf16[384,2048]{1,0:T(8,128)(2,1)S(1)} %pack.3.refs_0_), channel_id=1, source_target_pairs={{0,1},{1,0},{2,3},{3,2},{4,5},{5,4},{6,7},{7,6},{8,9},{9,8},{10,11... | collective-permute-start | bytes 4718600 | tf_op jit(solution)/shard_map/ppermute | solution.py:26
  59.6 36.4 %collective-permute-start.9 = (bf16[384,2048]{1,0:T(8,128)(2,1)S(1)}, bf16[384,2048]{1,0:T(8,128)(2,1)S(1)}, u32[]{:S(2)}, u32[]{:S(2)}) collective-permute-start(bf16[384,2048]{1,0:T(8,128)(2,1)S(1)} %pack.3.refs_0_), channel_id=1, source_target_pairs={{0,2},{1,3},{2,0},{3,1},{4,6},{5,7},{6,4},{7,5},{8,10},{9,11},{10,... | collective-permute-start | bytes 4718600 | tf_op jit(solution)/shard_map/ppermute | solution.py:26
  75.1 6.1 %copy-start = (f32[512,128]{1,0:T(8,128)}, f32[512,128]{1,0:T(8,128)S(1)}, u32[]{:S(2)}) copy-start(f32[512,128]{1,0:T(8,128)S(1)} %get-tuple-element.128.refs_0_) | copy-start | bytes 786436
  96.0 4.2 %collective-permute-start.11 = (bf16[384,2048]{1,0:T(8,128)(2,1)S(1)}, bf16[384,2048]{1,0:T(8,128)(2,1)S(1)}, u32[]{:S(2)}, u32[]{:S(2)}) collective-permute-start(bf16[384,2048]{1,0:T(8,128)(2,1)S(1)} %collective-permute-done.9.refs_0_), channel_id=1, source_target_pairs={{0,1},{1,0},{2,3},{3,2},{4,5},{5,4},{6,7},{7,6},{8,9},{9,8},{10,11... | collective-permute-start | bytes 4718600 | tf_op jit(solution)/shard_map/ppermute | solution.py:26
  107.5 0.7 copy-start.1
  108.2 15.4 %copy-start.11 = (f32[8,160]{1,0:T(8,128)S(1)}, f32[8,160]{1,0:T(8,128)}, u32[]{:S(2)}) copy-start(f32[8,160]{1,0:T(8,128)} %param.16) | copy-start | bytes 15364
  110.4 4.9 %collective-permute-start.12 = (f32[2,160]{1,0:T(2,128)}, f32[2,160]{1,0:T(2,128)S(1)}, u32[]{:S(2)}, u32[]{:S(2)}) collective-permute-start(f32[2,160]{1,0:T(2,128)} %get-tuple-element.159), channel_id=1, source_target_pairs={{0,4},{4,0},{8,12},{12,8},{16,20},{20,16},{24,28},{28,24},{1,5},{5... | collective-permute-start | bytes 3848 | tf_op jit(solution)/shard_map/ppermute | solution.py:26
  111.2 4.0 %collective-permute-start.14 = (f32[1,160]{1,0:T(1,128)}, f32[1,160]{1,0:T(1,128)S(1)}, u32[]{:S(2)}, u32[]{:S(2)}) collective-permute-start(f32[1,160]{1,0:T(1,128)} %get-tuple-element.161), channel_id=1, source_target_pairs={{0,8},{4,12},{8,0},{12,4},{16,24},{20,28},{24,16},{28,20},{1,9},{5... | collective-permute-start | bytes 1928 | tf_op jit(solution)/shard_map/ppermute | solution.py:26
  112.0 5.0 %collective-permute-start.13 = (f32[1,160]{1,0:T(1,128)}, f32[1,160]{1,0:T(1,128)S(1)}, u32[]{:S(2)}, u32[]{:S(2)}) collective-permute-start(f32[1,160]{1,0:T(1,128)} %get-tuple-element.160), channel_id=1, source_target_pairs={{0,16},{4,20},{8,24},{12,28},{16,0},{20,4},{24,8},{28,12},{1,17},{... | collective-permute-start | bytes 1928 | tf_op jit(solution)/shard_map/ppermute | solution.py:26
  117.8 1.2 collective-permute-start.15
  119.7 3.7 %collective-permute-start.16 = (f32[8,160]{1,0:T(8,128)S(1)}, f32[8,160]{1,0:T(8,128)S(1)}, u32[]{:S(2)}, u32[]{:S(2)}) collective-permute-start(f32[8,160]{1,0:T(8,128)S(1)} %fusion.29), channel_id=1, source_target_pairs={{0,2},{1,3},{2,0},{3,1},{4,6},{5,7},{6,4},{7,5},{8,10},{9,11},{10,... | collective-permute-start | bytes 15368 | tf_op jit(solution)/shard_map/ppermute | solution.py:26
  123.5 0.9 copy-start.10
where the time goes:
time: 125 us; the launch traced here: 124 us
  Pallas kernels  54.6 us (44%)
  waiting for transfers between devices  37.5 us (30%)
  starting transfers between devices  13.6 us (11%)
  blocking collectives  11.6 us (9%)
  other arithmetic  2.29 us (2%)
  local copies, waits for them, and re-layouts  2.24 us (2%)
  between operations  1.64 us (1%)
    ppermute x14, waiting for transfers between devices, swapped(): return lax.ppermute(value, axis, [(i, i ^ bit) for i in range(length)])  37.5 us
    pallas_call x2, Pallas kernels, attend_call(): pl.pallas_call(functools.partial(attend_kernel, slot, tile, begin, len(fl...  21.1 us
    pallas_call x3, Pallas kernels, sums_call(): pl.pallas_call(functools.partial(sums_kernel, len(flips), groups, begun i...  20 us
    ppermute x14, starting transfers between devices, swapped(): return lax.ppermute(value, axis, [(i, i ^ bit) for i in range(length)])  13.6 us
    psum x1, blocking collectives, local(): lax.psum(jnp.where(jnp.arange(owners)[:, None] == me, lengths[None, :], 0...  11.6 us
    pallas_call x1, Pallas kernels, local(): pl.pallas_call(functools.partial(first_pack_kernel, slot_blocks), in_spec...  3.97 us
    pallas_call x1, Pallas kernels, local(): pl.pallas_call(functools.partial(plan_kernel, slot_blocks, first // GRAIN...  3.78 us
    pallas_call x1, Pallas kernels, pack(): pl.pallas_call(functools.partial(pack_kernel, begin, slot_blocks), in_spe...  3.63 us
  transfers between devices with their start and end apart: 14, of which 6 were waited for; matrix products, arithmetic and copies ran while one was open for 1% of the time, Pallas kernels for 33%

commit v1 on v0

--- a/solution.py
+++ b/solution.py
@@ -82,9 +82,13 @@
     return (value * cosine + pltpu.roll(value, HD // 2, 1) * sine).astype(jnp.bfloat16)
 
 
-def attend_kernel(slot, tile, begin, parts, part_ref, place_ref, *refs):
+def attend_kernel(slot, tile, begin, parts, last, part_ref, place_ref, *refs):
+    if last:
+        info_ref, refs = refs[0], refs[1:]
     x_refs, refs = [[ref] for ref in refs[:parts]], refs[parts:]
     weights, refs = refs[:4], refs[4:]
+    if last:
+        (total_ref, line_ref, *back_refs, rows_ref), refs = refs[-3 - len(BITS) :], refs[: -3 - len(BITS)]
     (
         q_ref, kv_ref, ss_ref, vt_ref, cos_ref, sin_ref, folded_ref, key_in, val_in,
         out_ref, key_out, val_out, q_acc, kv_acc, ss_acc, cos_rows, sin_rows, place_rows, keys, vals,
@@ -162,6 +166,10 @@
             return carry
 
         lax.fori_loop(0, rows // tile, one_tile, 0, unroll=2)
+        if last:
+            rows_ref[:begin, :] = total_ref[...]
+            rows_ref[begin : begin + rows, :] = out_ref[...]
+            unpack(slot, info_ref, rows_ref, line_ref, back_refs)
 
 
 def start_copy(source, source_block, target, target_block, sem):
@@ -172,20 +180,8 @@
     ).start()
 
 
-def wait_copies(source, targets, sems):
-    begin = 0
-    for target in targets:
-
-        def wait(b, carry, target=target, begin=begin):
-            pltpu.make_async_copy(
-                source.at[pl.ds(0, GRAIN)],
-                target.at[pl.ds(pl.multiple_of(b * GRAIN, GRAIN), GRAIN)],
-                sems.at[begin + b],
-            ).wait()
-            return carry
-
-        lax.fori_loop(0, target.shape[0] // GRAIN, wait, 0)
-        begin += target.shape[0] // GRAIN
+def wait_copies(source, target, sem):
+    pltpu.make_async_copy(source.at[pl.ds(0, target.shape[0])], target, sem).wait()
 
 
 def blocks_of(length):
@@ -210,28 +206,31 @@
     lax.fori_loop(0, source_ref.shape[0], enter, 0)
 
 
-def first_pack_kernel(slot_blocks, lengths_ref, hidden_ref, place_ref, *refs):
-    outs, (source_ref, sems) = refs[:-2], refs[-2:]
-    lay_out_fill(slot_blocks, source_ref, place_ref)
+def first_pack_kernel(slot_blocks, lengths_ref, hidden_ref, place_ref, out_ref, sem):
+    total = out_ref.shape[0] // GRAIN
+
+    def copy(j, carry, at, first_block):
+        start_copy(hidden_ref, first_block + j, out_ref, at + j, sem)
+        place_ref[at + j] = j
+        return carry
+
     at = jnp.int32(0)
     for i in range(lengths_ref.shape[0]):
-        count = blocks_of(lengths_ref[i])
-        lay_out(at, count, slot_blocks, i * slot_blocks, source_ref, place_ref)
+        count = jnp.minimum(blocks_of(lengths_ref[i]), total - at)
+        lax.fori_loop(0, count, functools.partial(copy, at=at, first_block=i * slot_blocks), 0)
         at = at + count
-    begin = 0
-    for out_ref in outs:
-
-        def start(b, carry, out_ref=out_ref, begin=begin):
-            start_copy(hidden_ref, source_ref[begin + b], out_ref, b, sems.at[begin + b])
-            return carry
-
-        lax.fori_loop(0, out_ref.shape[0] // GRAIN, start, 0)
-        begin += out_ref.shape[0] // GRAIN
-    wait_copies(hidden_ref, outs, sems)
+
+    def fill(b, carry):
+        start_copy(hidden_ref, 0, out_ref, b, sem)
+        place_ref[b] = 0
+        return carry
+
+    lax.fori_loop(at, total, fill, 0)
+    wait_copies(hidden_ref, out_ref, sem)
 
 
 def plan_kernel(
-    slot_blocks, first_blocks, capacity, me_ref, lengths_ref, hidden_ref,
+    slot_blocks, first_blocks, capacity, extra, me_ref, lengths_ref, hidden_ref,
     source_ref, place_ref, info_ref, *refs,
 ):
     kept, load, sent, moved, sems = refs[len(BITS) :]
@@ -283,7 +282,8 @@
         lax.fori_loop(0, owners, move, 0)
 
     most = lax.fori_loop(0, owners, lambda o, m: jnp.maximum(m, load[o]), jnp.int32(0))
-    info_ref[OVERFLOW] = jnp.where(most > capacity, 1, 0)
+    more = jnp.where(most > capacity + extra, 2, 1)
+    info_ref[OVERFLOW] = jnp.where(most > capacity, more, 0)
 
     lay_out_fill(slot_blocks, source_ref, place_ref)
     at = jnp.int32(0)
@@ -303,55 +303,62 @@
 
 
 def pack_kernel(begin, slot_blocks, source_ref, hidden_ref, *refs):
-    outs, sems = refs[len(BITS) : -1], refs[-1]
+    out_ref, sem = refs[len(BITS) :]
     size = slot_blocks * GRAIN
     arrivals = [
         refs[BITS.index(bit)].at[pl.ds(ROUTES[:r].count(bit) * size, size)]
         for r, bit in enumerate(ROUTES)
     ]
     own = hidden_ref.shape[0] // GRAIN
-    done = 0
-    for out_ref in outs:
-
-        def start(b, carry, out_ref=out_ref, done=done):
-            block = source_ref[begin // GRAIN + done + b]
-
-            @pl.when(block < own)
-            def _():
-                start_copy(hidden_ref, block, out_ref, b, sems.at[done + b])
-
-            for r, arrival in enumerate(arrivals):
-                low = own + r * slot_blocks
-
-                @pl.when((block >= low) & (block < low + slot_blocks))
-                def _(arrival=arrival, low=low):
-                    start_copy(arrival, block - low, out_ref, b, sems.at[done + b])
-
-            return carry
-
-        lax.fori_loop(0, out_ref.shape[0] // GRAIN, start, 0)
-        done += out_ref.shape[0] // GRAIN
-    wait_copies(hidden_ref, outs, sems)
-
-
-def unpack_kernel(slot, rollouts, info_ref, *refs):
+
+    def start(b, carry):
+        block = source_ref[begin // GRAIN + b]
+
+        @pl.when(block < own)
+        def _():
+            start_copy(hidden_ref, block, out_ref, b, sem)
+
+        for r, arrival in enumerate(arrivals):
+            low = own + r * slot_blocks
+
+            @pl.when((block >= low) & (block < low + slot_blocks))
+            def _(arrival=arrival, low=low):
+                start_copy(arrival, block - low, out_ref, b, sem)
+
+        return carry
+
+    lax.fori_loop(0, out_ref.shape[0] // GRAIN, start, 0)
+    wait_copies(hidden_ref, out_ref, sem)
+
+
+def unpack(slot, info_ref, rows_ref, out_ref, back_refs):
+    rollouts = out_ref.shape[0]
+
+    def line(block):
+        part = rows_ref[pl.ds(pl.multiple_of(block * GRAIN, GRAIN), 2 * HD), :]
+        return jnp.sum(part.T, axis=0, keepdims=True)[:, :slot]
+
+    for i in range(rollouts):
+        out_ref[i : i + 1, :] = line(info_ref[SLOT_AT + i])
+    for r, bit in enumerate(ROUTES):
+        back_ref, i = back_refs[BITS.index(bit)], ROUTES[:r].count(bit)
+        back_ref[i : i + 1, :] = line(info_ref[ARRIVED_AT + r])
+
+
+def unpack_kernel(slot, info_ref, *refs):
     totals, out_ref, back_refs, rows_ref = refs[:3], refs[3], refs[4:-1], refs[-1]
     at = 0
     for total in totals:
         rows_ref[at : at + total.shape[0], :] = total[...]
         at += total.shape[0]
     rows_ref[at:, :] = jnp.zeros((rows_ref.shape[0] - at, HD), jnp.float32)
-    span = rows_ref.shape[0] - at
-
-    def line(block):
-        part = rows_ref[pl.ds(pl.multiple_of(block * GRAIN, GRAIN), span), :]
-        return jnp.sum(part.T, axis=0, keepdims=True)[:, :slot]
-
-    for i in range(rollouts):
-        out_ref[i : i + 1, :] = line(info_ref[SLOT_AT + i])
-    for r, bit in enumerate(ROUTES):
-        back_ref, i = back_refs[BITS.index(bit)], ROUTES[:r].count(bit)
-        back_ref[i : i + 1, :] = line(info_ref[ARRIVED_AT + r])
+    unpack(slot, info_ref, rows_ref, out_ref, back_refs)
+
+
+def line_shapes(rollouts, slot):
+    return [jax.ShapeDtypeStruct((rollouts, slot), jnp.float32)] + [
+        jax.ShapeDtypeStruct((ROUTES.count(bit), slot), jnp.float32) for bit in BITS
+    ]
 
 
 def weight_specs(flips, blocks, widths):
@@ -410,22 +417,44 @@
     return [sums[4 * g : 4 * g + 4] for g in range(groups)]
 
 
-def attend_call(shared, tables, begin, places, flips, xs, sums, before):
+def attend_call(shared, tables, begin, places, flips, xs, sums, before, last=None):
     part, gain, weights = shared
     widths = [w.shape[1] for w in weights]
     count, blocks = xs[0].shape[0], xs[0].shape[1] // DEPTH
     slot = tables[0].shape[0]
-    tile = max(t for t in range(GRAIN, slot // 2 + 1, GRAIN) if count % t == 0)
+    tile = max(t for t in range(GRAIN, 97, GRAIN) if count % t == 0)
     stacked = widths[0] // HD * tile
+    scalars, given, lines, space = [part, places], [], [], []
+    if last:
+        info, ahead, rollouts, rows = last
+        scalars, given, lines = [*scalars, info], [ahead], line_shapes(rollouts, slot)
+        space = [pltpu.VMEM((rows + 2 * HD, HD), jnp.float32)]
+    outs = [
+        jax.ShapeDtypeStruct((count, HD), jnp.float32),
+        jax.ShapeDtypeStruct((slot, HD), jnp.bfloat16),
+        jax.ShapeDtypeStruct((slot, HD), jnp.bfloat16),
+    ]
+
+    def kernel(*refs):
+        n = len(scalars) + len(flips) + 4 + len(sums) + len(tables) + len(before)
+        inputs, more, refs = refs[:n], refs[n : n + len(given)], refs[n + len(given) :]
+        own, rest = refs[: len(outs)], refs[len(outs) :]
+        extra, scratch = rest[: len(lines)], rest[len(lines) :]
+        scratch, room = scratch[: len(scratch) - len(space)], scratch[len(scratch) - len(space) :]
+        attend_kernel(
+            slot, tile, begin, len(flips), last is not None,
+            *inputs, *own, *scratch, *more, *extra, *room,
+        )
+
     return pl.pallas_call(
-        functools.partial(attend_kernel, slot, tile, begin, len(flips)),
+        kernel,
         grid_spec=pltpu.PrefetchScalarGridSpec(
-            num_scalar_prefetch=2,
+            num_scalar_prefetch=len(scalars),
             grid=(len(flips) * blocks,),
             in_specs=[x_spec(count, blocks, f) for f in range(len(flips))]
             + weight_specs(flips, blocks, widths)
-            + [fixed(*a.shape) for a in (*sums, *tables, *before)],
-            out_specs=[fixed(count, HD), fixed(slot, HD), fixed(slot, HD)],
+            + [fixed(*a.shape) for a in (*sums, *tables, *before, *given)],
+            out_specs=[fixed(*a.shape) for a in (*outs, *lines)],
             scratch_shapes=[
                 pltpu.VMEM((count, widths[0]), jnp.float32),
                 pltpu.VMEM((count, widths[1] + widths[2]), jnp.float32),
@@ -438,17 +467,14 @@
                 pltpu.VMEM((stacked, HD), jnp.bfloat16),
                 pltpu.VMEM((stacked, slot + tile), jnp.bfloat16),
                 pltpu.VMEM((DEPTH, 2 * HD), jnp.bfloat16),
-            ],
+            ]
+            + space,
         ),
-        out_shape=[
-            jax.ShapeDtypeStruct((count, HD), jnp.float32),
-            jax.ShapeDtypeStruct((slot, HD), jnp.bfloat16),
-            jax.ShapeDtypeStruct((slot, HD), jnp.bfloat16),
-        ],
+        out_shape=outs + lines,
         compiler_params=pltpu.CompilerParams(vmem_limit_bytes=24 << 20),
         cost_estimate=cost(count, len(flips) * blocks * DEPTH, sum(widths)),
         name="attend",
-    )(part, places, *xs, gain, *weights, *sums, *tables, *before)
+    )(*scalars, *xs, gain, *weights, *sums, *tables, *before, *given)
 
 
 def local(
@@ -482,8 +508,9 @@
 
     slot_blocks = slot // GRAIN
     packed = segment_ids.shape[0]
-    first = packed * 4 // 5
-    second = packed * 3 // 5
+    first = packed * 7 // 8
+    second = packed // 2
+    extra = packed // 8
     rest = rows - first - second
     whole = jax.ShapeDtypeStruct
     anywhere = pl.BlockSpec(memory_space=pl.ANY)
@@ -499,11 +526,8 @@
         functools.partial(first_pack_kernel, slot_blocks),
         in_specs=[scalars, anywhere],
         out_specs=[scalars, onchip],
-        out_shape=[whole((blocks_in_all,), jnp.int32), whole((first, part_width), hidden.dtype)],
-        scratch_shapes=[
-            pltpu.SMEM((blocks_in_all,), jnp.int32),
-            pltpu.SemaphoreType.DMA((first // GRAIN,)),
-        ],
+        out_shape=[whole((first // GRAIN,), jnp.int32), whole((first, part_width), hidden.dtype)],
+        scratch_shapes=[pltpu.SemaphoreType.DMA],
         compiler_params=vmem,
         name="first_pack",
     )(lengths, hidden)
@@ -517,7 +541,7 @@
     ).reshape(-1)
     source, places, info, *ships = pl.pallas_call(
         functools.partial(
-            plan_kernel, slot_blocks, first // GRAIN, (first + second) // GRAIN
+            plan_kernel, slot_blocks, first // GRAIN, (first + second) // GRAIN, extra // GRAIN
         ),
         in_specs=[scalars, scalars, anywhere],
         out_specs=[scalars, scalars, scalars] + [onchip] * len(BITS),
@@ -544,7 +568,7 @@
             in_specs=[scalars, anywhere] + [anywhere] * len(BITS),
             out_specs=onchip,
             out_shape=whole((count, part_width), hidden.dtype),
-            scratch_shapes=[pltpu.SemaphoreType.DMA((count // GRAIN,))],
+            scratch_shapes=[pltpu.SemaphoreType.DMA],
             compiler_params=vmem,
             name="pack",
         )(source, hidden, *arrivals)
@@ -557,10 +581,11 @@
     nothing = jnp.zeros((slot, HD), jnp.bfloat16)
     before = (nothing, nothing)
     (sums_first,) = sums_call(shared, (0, 1), [[x_first], [near_first]], head)
-    far_first, mine, sums_first, *arrivals = lax.optimization_barrier(
-        (far_first, mine, sums_first, *arrivals)
+    mine, over, sums_first, *arrivals = lax.optimization_barrier(
+        (mine, info[OVERFLOW], sums_first, *arrivals)
     )
     x_second = pack(first, second)
+    far_first, x_second = lax.optimization_barrier((far_first, x_second))
     far_second = swapped(x_second, "mp", 2)
     near_second = swapped(x_second, "mp", 1)
     total_first, *before = attend(0, places_first, far_first, sums_first, before)
@@ -570,28 +595,27 @@
     far_near = swapped(far_second, "mp", 1)
     (sums_second,) = sums_call(shared, (2,), [[far_second]], head, begun=[sums_second])
     far_near, sums_second = lax.optimization_barrier((far_near, sums_second))
-    total_second, *before = attend_call(
-        shared, tables, first, places, (3,), [far_near], sums_second, before
+    total_second, key_rows, val_rows, *lines = attend_call(
+        shared, tables, first, places, (3,), [far_near], sums_second, before,
+        last=(info, total_first, rollouts, rows),
     )
 
-    def overflow(before):
+    def overflow(count, _):
         begin = first + second
-        x = pack(begin, rest)
+        x = pack(begin, count)
         (sums,) = sums_call(shared, (0, 1), [[x], [swapped(x, "mp", 1)]], head)
-        return attend(begin, places, swapped(x, "mp", 2), sums, before)[0]
-
-    total_rest = lax.cond(
-        info[OVERFLOW] > 0, overflow, lambda _: jnp.zeros((rest, HD), jnp.float32), before
-    )
-    totals = (total_first, total_second, total_rest)
-    slot_terms, *backs = pl.pallas_call(
-        functools.partial(unpack_kernel, slot, rollouts),
-        in_specs=[scalars] + [onchip] * len(totals),
-        out_shape=[whole((rollouts, slot), jnp.float32)]
-        + [whole((ROUTES.count(bit), slot), jnp.float32) for bit in BITS],
-        scratch_shapes=[pltpu.VMEM((rows + 2 * HD, HD), jnp.float32)],
-        name="unpack",
-    )(info, *totals)
+        far = swapped(x, "mp", 2)
+        total_rest, *_ = attend(begin, places, far, sums, (key_rows, val_rows))
+        return tuple(pl.pallas_call(
+            functools.partial(unpack_kernel, slot),
+            in_specs=[scalars] + [onchip] * 3,
+            out_shape=line_shapes(rollouts, slot),
+            scratch_shapes=[pltpu.VMEM((rows + 2 * HD, HD), jnp.float32)],
+            name="unpack",
+        )(info, total_first, total_second, total_rest))
+
+    more = [functools.partial(overflow, count) for count in (extra, rest)]
+    slot_terms, *backs = lax.switch(over, [tuple, *more], lines)
     backs = [swapped(back, "dp", bit) for back, bit in zip(backs, BITS, strict=True)]
     for r, bit in enumerate(ROUTES):
         back = backs[BITS.index(bit)][ROUTES[:r].count(bit)]

time: 125 us -> 117 us (0.936)
  waiting for transfers between devices: 37.5 us -> 29.4 us
  starting transfers between devices: 13.6 us -> 15.3 us
  other arithmetic: 2.29 us -> 0.9 us
  Pallas kernels: 54.6 us -> 55.9 us
    ppermute x14, waiting for transfers between devices: 37.5 us -> 29.4 us  [swapped(): return lax.ppermute(value, axis, [(i, i ^ bit) for i in range(length)])]
    pallas_call x3, Pallas kernels: 20 us -> 22.5 us  [sums_call(): pl.pallas_call(functools.partial(sums_kernel, len(flips), groups, begun i...]
    ppermute x14, starting transfers between devices: 13.6 us -> 15.3 us  [swapped(): return lax.ppermute(value, axis, [(i, i ^ bit) for i in range(length)])]
    pallas_call x3 -> x2, Pallas kernels: 23.2 us -> 23.1 us  [attend_call(): pl.pallas_call(kernel, grid_spec=pltpu.PrefetchScalarGridSpec(num_scalar_...]
  transfers between devices with their start and end apart: 14 -> 14, of which waited for: 6 -> 8; matrix products, arithmetic and copies ran while one was open for 1% -> 1% of each run, Pallas kernels for 33% -> 38%
where the time goes in v1:
time: 117 us
  Pallas kernels  55.9 us (48%)
  waiting for transfers between devices  29.4 us (25%)
  starting transfers between devices  15.3 us (13%)
  blocking collectives  11.6 us (10%)
  between operations  1.55 us (1%)
  local copies, waits for them, and re-layouts  1.54 us (1%)
    ppermute x14, waiting for transfers between devices, swapped(): return lax.ppermute(value, axis, [(i, i ^ bit) for i in range(length)])  29.4 us
    pallas_call x2, Pallas kernels, attend_call(): pl.pallas_call(kernel, grid_spec=pltpu.PrefetchScalarGridSpec(num_scalar_...  23.1 us
    pallas_call x3, Pallas kernels, sums_call(): pl.pallas_call(functools.partial(sums_kernel, len(flips), groups, begun i...  22.5 us
    ppermute x14, starting transfers between devices, swapped(): return lax.ppermute(value, axis, [(i, i ^ bit) for i in range(length)])  15.3 us
    psum x1, blocking collectives, local(): lax.psum(jnp.where(jnp.arange(owners)[:, None] == me, lengths[None, :], 0...  11.6 us
    pallas_call x1, Pallas kernels, local(): pl.pallas_call(functools.partial(plan_kernel, slot_blocks, first // GRAIN...  3.89 us
    pallas_call x1, Pallas kernels, local(): pl.pallas_call(functools.partial(first_pack_kernel, slot_blocks), in_spec...  3.62 us
    pallas_call x1, Pallas kernels, pack(): pl.pallas_call(functools.partial(pack_kernel, begin, slot_blocks), in_spe...  2.72 us
  transfers between devices with their start and end apart: 14, of which 8 were waited for; matrix products, arithmetic and copies ran while one was open for 1% of the time, Pallas kernels for 38%

profile of v1, /device:TPU:0, one launch (start us, length us, event | category | flops | bytes accessed | tf_op | source)
XLA Modules:
  0.0 117.1 jit_solution(13578882308716276918)
XLA Ops:
  0.6 0.6 copy-done.2
  1.3 3.6 %first_pack.1 = (s32[35]{0:T(128)S(1)}, bf16[560,2048]{1,0:T(8,128)(2,1)}) custom-call(s32[8]{0:T(128)S(1)} %copy-done.2, bf16[1280,2048]{1,0:T(8,128)(2,1)} %hidden_ref.5), custom_call_target="tpu_custom_call" | custom-call | tf_op jit(solution)/shard_map/first_pack/pallas_call | solution.py:525
  4.9 0.5 collective-permute-start.6
  5.4 2.6 %collective-permute-start.10 = (bf16[560,2048]{1,0:T(8,128)(2,1)}, bf16[560,2048]{1,0:T(8,128)(2,1)S(1)}, u32[]{:S(2)}, u32[]{:S(2)}) collective-permute-start(bf16[560,2048]{1,0:T(8,128)(2,1)} %get-tuple-element.198.refs_0_), channel_id=1, source_target_pairs={{0,2},{1,3},{2,0},{3,1},{4,6},{5,7},{6,4},{7,5},{8,10},{9,11},{10,... | collective-permute-start | bytes 6881288 | tf_op jit(solution)/shard_map/ppermute | solution.py:26
  8.0 0.1 broadcast_select_fusion
  8.1 0.1 reshape.34
  8.2 11.6 %psum.7.lengths_ref = s32[64]{0:T(128)S(1)} all-reduce(s32[64]{0:T(128)S(1)} %reshape.34), channel_id=1, replica_groups=mesh['dp'=8,'mp'=4] {'dp'}, use_global_device_ids=true, to_apply=%region_0.1 | all-reduce | flops 64 | bytes 512 | tf_op jit(solution)/shard_map/psum | solution.py:539
  19.8 3.9 %plan.1 = (s32[80]{0:T(128)S(1)}, s32[80]{0:T(128)S(1)}, s32[64]{0:T(128)S(1)}, bf16[320,2048]{1,0:T(8,128)(2,1)}, bf16[160,2048]{1,0:T(8,128)(2,1)}, /*index=5*/bf16[160,2048]{1,0:T(8,128)(2,1)S(1)}) custom-call(s32[1]{0:T(128)} %bitcast.me_ref, s32[64]{0:T(128)S(1)} %psum.7.lengths_ref, bf16[1280,2048]{1,0:T(8,128)(2,1)} %hidden_ref.5), custom_call_target="tpu_custom_call" | custom-call | tf_op jit(solution)/shard_map/plan/pallas_call | solution.py:542
  23.7 1.6 %collective-permute-start.7 = (bf16[320,2048]{1,0:T(8,128)(2,1)}, bf16[320,2048]{1,0:T(8,128)(2,1)}, u32[]{:S(2)}, u32[]{:S(2)}) collective-permute-start(bf16[320,2048]{1,0:T(8,128)(2,1)} %get-tuple-element.203), channel_id=1, source_target_pairs={{0,4},{4,0},{8,12},{12,8},{16,20},{20,16},{24,28},{28,24},{1,5},{5... | collective-permute-start | bytes 3932168 | tf_op jit(solution)/shard_map/ppermute | solution.py:26
  25.3 0.5 collective-permute-start.8
  25.8 0.3 collective-permute-start.9
  26.1 0.1 slice.31
  26.2 0.1 slice_compare_fusion
  26.3 0.1 fusion.24
  26.3 0.6 slice.32
  27.0 0.0 slice-start
  27.0 0.0 slice-start.1
  27.0 11.8 %sums.7 = (f32[560,1024]{1,0:T(8,128)S(1)}, f32[560,256]{1,0:T(8,128)S(1)}, f32[560,128]{1,0:T(8,128)S(1)}, f32[560,128]{1,0:T(8,128)S(1)}) custom-call(s32[1]{0:T(128)} %bitcast.2.part_ref.refs_0_, bf16[560,2048]{1,0:T(8,128)(2,1)} %get-tuple-element.198.refs_0_, bf16[560,2048]{1,0:T(8,128)(2,1)} %collective-permute-done.6.refs_1_, f32[1,8192]{1,0:T(1,128)S(1)} %bitcast.24, ...), custom_call_target="tpu_custom_call" | custom-call | flops 5872025600 | bytes 17940480 | tf_op jit(solution)/shard_map/sums/pallas_call | solution.py:400
  38.8 14.0 %collective-permute-done.8.refs_1_ = bf16[160,2048]{1,0:T(8,128)(2,1)} collective-permute-done((bf16[160,2048]{1,0:T(8,128)(2,1)}, bf16[160,2048]{1,0:T(8,128)(2,1)}, u32[]{:S(2)}, u32[]{:S(2)}) %collective-permute-start.8) | collective-permute-done | bytes 655392 | tf_op jit(solution)/shard_map/ppermute | solution.py:26
  52.8 2.0 %collective-permute-done.9.refs_2_ = bf16[160,2048]{1,0:T(8,128)(2,1)} collective-permute-done((bf16[160,2048]{1,0:T(8,128)(2,1)S(1)}, bf16[160,2048]{1,0:T(8,128)(2,1)}, u32[]{:S(2)}, u32[]{:S(2)}) %collective-permute-start.9) | collective-permute-done | bytes 655392 | tf_op jit(solution)/shard_map/ppermute | solution.py:26
  54.8 0.0 slice-start.3
  54.9 0.0 copy-start.12
  54.9 2.7 %pack.5.refs_0_ = bf16[320,2048]{1,0:T(8,128)(2,1)S(1)} custom-call(s32[80]{0:T(128)S(1)} %get-tuple-element.209.source_ref, bf16[1280,2048]{1,0:T(8,128)(2,1)S(1)} %bitcast.23, bf16[320,2048]{1,0:T(8,128)(2,1)} %collective-permute-done.7.refs_0_, bf16[160,2048]{1,0:T(8,128)(2,1)} %collective-permute-done.8.refs_1_, ...), custom_call_target="tpu_custom_call" | custom-call | tf_op jit(solution)/shard_map/pack/pallas_call | solution.py:566
  57.6 1.1 collective-permute-done.10.refs_2_
  58.7 0.5 collective-permute-start.12
  59.2 1.8 %collective-permute-start.11 = (bf16[320,2048]{1,0:T(8,128)(2,1)S(1)}, bf16[320,2048]{1,0:T(8,128)(2,1)}, u32[]{:S(2)}, u32[]{:S(2)}) collective-permute-start(bf16[320,2048]{1,0:T(8,128)(2,1)S(1)} %pack.5.refs_0_), channel_id=1, source_target_pairs={{0,2},{1,3},{2,0},{3,1},{4,6},{5,7},{6,4},{7,5},{8,10},{9,11},{10,... | collective-permute-start | bytes 3932168 | tf_op jit(solution)/shard_map/ppermute | solution.py:26
  61.0 0.3 fusion.12
  61.3 0.1 pad_maximum_fusion
  61.4 1.7 %collective-permute-done.13.refs_3_ = bf16[560,2048]{1,0:T(8,128)(2,1)S(1)} collective-permute-done((bf16[560,2048]{1,0:T(8,128)(2,1)S(1)}, bf16[560,2048]{1,0:T(8,128)(2,1)S(1)}, u32[]{:S(2)}, u32[]{:S(2)}) %collective-permute-start.13) | collective-permute-done | bytes 2293792 | tf_op jit(solution)/shard_map/ppermute | solution.py:26
  63.2 15.1 %attend.6 = (f32[560,128]{1,0:T(8,128)}, bf16[160,128]{1,0:T(8,128)(2,1)S(1)}, bf16[160,128]{1,0:T(8,128)(2,1)S(1)}) custom-call(s32[1]{0:T(128)} %bitcast.2.part_ref.refs_0_, s32[35]{0:T(128)S(1)} %get-tuple-element.214.refs_1_, bf16[560,2048]{1,0:T(8,128)(2,1)S(1)} %collective-permute-done.10.refs_2_, ...), custom_call_target="tpu_custom_call" | custom-call | flops 5872025600 | bytes 17940480 | tf_op jit(solution)/shard_map/attend/pallas_call | solution.py:449
  78.3 6.3 %sums.8 = (f32[320,1024]{1,0:T(8,128)S(1)}, f32[320,256]{1,0:T(8,128)S(1)}, f32[320,128]{1,0:T(8,128)S(1)}, f32[320,128]{1,0:T(8,128)S(1)}) custom-call(s32[1]{0:T(128)} %bitcast.2.part_ref.refs_0_, bf16[320,2048]{1,0:T(8,128)(2,1)S(1)} %pack.5.refs_0_, bf16[320,2048]{1,0:T(8,128)(2,1)S(1)} %collective-permute-done.12.refs_1_, f32[1,8192]{1,0:T(1,128)S(1)} %bitcast.26, ...), custom_call_target="tpu_custom_call" | custom-call | flops 3355443200 | bytes 14745600 | tf_op jit(solution)/shard_map/sums/pallas_call | solution.py:400
  84.6 5.4 %collective-permute-done.11.refs_0_ = bf16[320,2048]{1,0:T(8,128)(2,1)} collective-permute-done((bf16[320,2048]{1,0:T(8,128)(2,1)S(1)}, bf16[320,2048]{1,0:T(8,128)(2,1)}, u32[]{:S(2)}, u32[]{:S(2)}) %collective-permute-start.11) | collective-permute-done | bytes 1310752 | tf_op jit(solution)/shard_map/ppermute | solution.py:26
  90.7 4.5 %sums.9 = (f32[320,1024]{1,0:T(8,128)S(1)}, f32[320,256]{1,0:T(8,128)S(1)}, f32[320,128]{1,0:T(8,128)S(1)}, f32[320,128]{1,0:T(8,128)S(1)}) custom-call(s32[1]{0:T(128)} %bitcast.2.part_ref.refs_0_, bf16[320,2048]{1,0:T(8,128)(2,1)} %collective-permute-done.11.refs_0_, f32[1,8192]{1,0:T(1,128)S(1)} %bitcast.27, bf16[8192,1024]{1,0:T(8,128)(2,1)} %refs_5_.7, ...), custom_call_target="tpu_custom_call" | custom-call | flops 1677721600 | bytes 8192000 | tf_op jit(solution)/shard_map/sums/pallas_call | solution.py:400
  95.1 8.0 %attend.7 = (f32[320,128]{1,0:T(8,128)S(1)}, bf16[160,128]{1,0:T(8,128)(2,1)S(1)}, bf16[160,128]{1,0:T(8,128)(2,1)S(1)}, f32[8,160]{1,0:T(8,128)S(1)}, f32[2,160...) custom-call(s32[1]{0:T(128)} %bitcast.2.part_ref.refs_0_, s32[80]{0:T(128)S(1)} %get-tuple-element.208.refs_1_, ...), custom_call_target="tpu_custom_call" | custom-call | flops 1677721600 | bytes 8192000 | tf_op jit(solution)/shard_map/attend/pallas_call | solution.py:449
  103.2 0.0 copy-start.14
  103.2 1.8 %collective-permute-start.15 = (f32[2,160]{1,0:T(2,128)S(1)}, f32[2,160]{1,0:T(2,128)S(1)}, u32[]{:S(2)}, u32[]{:S(2)}) collective-permute-start(f32[2,160]{1,0:T(2,128)S(1)} %get-tuple-element.250), channel_id=1, source_target_pairs={{0,4},{4,0},{8,12},{12,8},{16,20},{20,16},{24,28},{28,24},{1,5},{5... | collective-permute-start | bytes 3848 | tf_op jit(solution)/shard_map/ppermute | solution.py:26
  105.0 1.6 %collective-permute-start.17 = (f32[1,160]{1,0:T(1,128)S(1)}, f32[1,160]{1,0:T(1,128)S(1)}, u32[]{:S(2)}, u32[]{:S(2)}) collective-permute-start(f32[1,160]{1,0:T(1,128)S(1)} %get-tuple-element.252), channel_id=1, source_target_pairs={{0,8},{4,12},{8,0},{12,4},{16,24},{20,28},{24,16},{28,20},{1,9},{5... | collective-permute-start | bytes 1928 | tf_op jit(solution)/shard_map/ppermute | solution.py:26
  106.6 2.6 %collective-permute-start.16 = (f32[1,160]{1,0:T(1,128)S(1)}, f32[1,160]{1,0:T(1,128)S(1)}, u32[]{:S(2)}, u32[]{:S(2)}) collective-permute-start(f32[1,160]{1,0:T(1,128)S(1)} %get-tuple-element.251), channel_id=1, source_target_pairs={{0,16},{4,20},{8,24},{12,28},{16,0},{20,4},{24,8},{28,12},{1,17},{... | collective-permute-start | bytes 1928 | tf_op jit(solution)/shard_map/ppermute | solution.py:26
  109.2 1.9 %collective-permute-done.16 = f32[1,160]{1,0:T(1,128)S(1)} collective-permute-done((f32[1,160]{1,0:T(1,128)S(1)}, f32[1,160]{1,0:T(1,128)S(1)}, u32[]{:S(2)}, u32[]{:S(2)}) %collective-permute-start.16) | collective-permute-done | bytes 672 | tf_op jit(solution)/shard_map/ppermute | solution.py:26
  111.1 0.1 select_select_fusion
  111.2 0.0 collective-permute-start.18
  111.2 1.2 collective-permute-done.18
  112.3 0.1 fusion.29
  112.4 1.5 %collective-permute-start.19 = (f32[8,160]{1,0:T(8,128)S(1)}, f32[8,160]{1,0:T(8,128)S(1)}, u32[]{:S(2)}, u32[]{:S(2)}) collective-permute-start(f32[8,160]{1,0:T(8,128)S(1)} %fusion.29), channel_id=1, source_target_pairs={{0,2},{1,3},{2,0},{3,1},{4,6},{5,7},{6,4},{7,5},{8,10},{9,11},{10,... | collective-permute-start | bytes 15368 | tf_op jit(solution)/shard_map/ppermute | solution.py:26
  113.9 2.1 %collective-permute-done.19 = f32[8,160]{1,0:T(8,128)S(1)} collective-permute-done((f32[8,160]{1,0:T(8,128)S(1)}, f32[8,160]{1,0:T(8,128)S(1)}, u32[]{:S(2)}, u32[]{:S(2)}) %collective-permute-start.19) | collective-permute-done | bytes 5152 | tf_op jit(solution)/shard_map/ppermute | solution.py:26
  116.1 0.1 add_select_fusion
  116.1 0.1 slice.42
  116.2 0.8 fusion
  (39 shorter events, 0.1 us)
Async XLA Ops:
  0.6 0.7 copy-start.2
  1.3 6.8 %copy-start.3 = (s32[8]{0:T(128)S(1)}, s32[8]{0:T(128)}, u32[]{:S(2)}) copy-start(s32[8]{0:T(128)} %lengths_ref.1) | copy-start | bytes 100
  4.9 22.0 %collective-permute-start.6 = (bf16[560,2048]{1,0:T(8,128)(2,1)}, bf16[560,2048]{1,0:T(8,128)(2,1)}, u32[]{:S(2)}, u32[]{:S(2)}) collective-permute-start(bf16[560,2048]{1,0:T(8,128)(2,1)} %get-tuple-element.198.refs_0_), channel_id=1, source_target_pairs={{0,1},{1,0},{2,3},{3,2},{4,5},{5,4},{6,7},{7,6},{8,9},{9,8},{10,11... | collective-permute-start | bytes 6881288 | tf_op jit(solution)/shard_map/ppermute | solution.py:26
  5.4 53.2 %collective-permute-start.10 = (bf16[560,2048]{1,0:T(8,128)(2,1)}, bf16[560,2048]{1,0:T(8,128)(2,1)S(1)}, u32[]{:S(2)}, u32[]{:S(2)}) collective-permute-start(bf16[560,2048]{1,0:T(8,128)(2,1)} %get-tuple-element.198.refs_0_), channel_id=1, source_target_pairs={{0,2},{1,3},{2,0},{3,1},{4,6},{5,7},{6,4},{7,5},{8,10},{9,11},{10,... | collective-permute-start | bytes 6881288 | tf_op jit(solution)/shard_map/ppermute | solution.py:26
  19.8 7.1 %copy-start.5 = (f32[8192]{0:T(1024)S(1)}, f32[8192]{0:T(1024)}, u32[]{:S(2)}) copy-start(f32[8192]{0:T(1024)} %param.19) | copy-start | bytes 98308
  19.8 7.1 %copy-start.11 = (f32[2048]{0:T(1024)S(1)}, f32[2048]{0:T(1024)}, u32[]{:S(2)}) copy-start(f32[2048]{0:T(1024)} %param.23) | copy-start | bytes 24580
  23.7 31.1 %collective-permute-start.7 = (bf16[320,2048]{1,0:T(8,128)(2,1)}, bf16[320,2048]{1,0:T(8,128)(2,1)}, u32[]{:S(2)}, u32[]{:S(2)}) collective-permute-start(bf16[320,2048]{1,0:T(8,128)(2,1)} %get-tuple-element.203), channel_id=1, source_target_pairs={{0,4},{4,0},{8,12},{12,8},{16,20},{20,16},{24,28},{28,24},{1,5},{5... | collective-permute-start | bytes 3932168 | tf_op jit(solution)/shard_map/ppermute | solution.py:26
  25.3 27.5 %collective-permute-start.8 = (bf16[160,2048]{1,0:T(8,128)(2,1)}, bf16[160,2048]{1,0:T(8,128)(2,1)}, u32[]{:S(2)}, u32[]{:S(2)}) collective-permute-start(bf16[160,2048]{1,0:T(8,128)(2,1)} %get-tuple-element.204), channel_id=1, source_target_pairs={{0,8},{4,12},{8,0},{12,4},{16,24},{20,28},{24,16},{28,20},{1,9},{5... | collective-permute-start | bytes 1966088 | tf_op jit(solution)/shard_map/ppermute | solution.py:26
  25.8 29.0 %collective-permute-start.9 = (bf16[160,2048]{1,0:T(8,128)(2,1)S(1)}, bf16[160,2048]{1,0:T(8,128)(2,1)}, u32[]{:S(2)}, u32[]{:S(2)}) collective-permute-start(bf16[160,2048]{1,0:T(8,128)(2,1)S(1)} %get-tuple-element.205), channel_id=1, source_target_pairs={{0,16},{4,20},{8,24},{12,28},{16,0},{20,4},{24,8},{28,12},{1,17},{... | collective-permute-start | bytes 1966088 | tf_op jit(solution)/shard_map/ppermute | solution.py:26
  26.9 27.9 %slice-start.8 = ((s8[5242880]{0:T(1024)(128)(4,1)}), s8[4194304]{0:T(1024)(128)(4,1)S(1)}, s32[]{:S(2)}) async-start(s8[5242880]{0:T(1024)(128)(4,1)} %bitcast.22), calls=%async_computation.8 | async-start | bytes 8388608
  26.9 27.9 %slice-start.9 = ((s8[5242880]{0:T(1024)(128)(4,1)}), s8[1048576]{0:T(1024)(128)(4,1)S(1)}, s32[]{:S(2)}) async-start(s8[5242880]{0:T(1024)(128)(4,1)} %bitcast.22), calls=%async_computation.9 | async-start | bytes 2097152
  27.0 36.2 %slice-start = ((s8[16777216]{0:T(1024)(128)(4,1)}), s8[4194304]{0:T(1024)(128)(4,1)S(1)}, s32[]{:S(2)}) async-start(s8[16777216]{0:T(1024)(128)(4,1)} %bitcast.18), calls=%async_computation | async-start | bytes 8388608
  27.0 36.2 %slice-start.1 = ((s8[16777216]{0:T(1024)(128)(4,1)}), s8[4194304]{0:T(1024)(128)(4,1)S(1)}, s32[]{:S(2)}) async-start(s8[16777216]{0:T(1024)(128)(4,1)} %bitcast.18), calls=%async_computation.1 | async-start | bytes 8388608
  27.0 36.2 %slice-start.2 = ((s8[16777216]{0:T(1024)(128)(4,1)}), s8[4194304]{0:T(1024)(128)(4,1)S(1)}, s32[]{:S(2)}) async-start(s8[16777216]{0:T(1024)(128)(4,1)} %bitcast.18), calls=%async_computation.2 | async-start | bytes 8388608
  54.8 8.3 %slice-start.3 = ((s8[16777216]{0:T(1024)(128)(4,1)}), s8[4194304]{0:T(1024)(128)(4,1)S(1)}, s32[]{:S(2)}) async-start(s8[16777216]{0:T(1024)(128)(4,1)} %bitcast.18), calls=%async_computation.3 | async-start | bytes 8388608
  54.9 8.3 %copy-start.12 = (f32[1024]{0:T(1024)S(1)}, f32[1024]{0:T(1024)}, u32[]{:S(2)}) copy-start(f32[1024]{0:T(1024)} %param.24) | copy-start | bytes 12292
  58.7 4.4 %collective-permute-start.13 = (bf16[560,2048]{1,0:T(8,128)(2,1)S(1)}, bf16[560,2048]{1,0:T(8,128)(2,1)S(1)}, u32[]{:S(2)}, u32[]{:S(2)}) collective-permute-start(bf16[560,2048]{1,0:T(8,128)(2,1)S(1)} %collective-permute-done.10.refs_2_), channel_id=1, source_target_pairs={{0,1},{1,0},{2,3},{3,2},{4,5},{5,4},{6,7},{7,6},{8,9},{9,8},{10,11... | collective-permute-start | bytes 6881288 | tf_op jit(solution)/shard_map/ppermute | solution.py:26
  58.7 19.6 %collective-permute-start.12 = (bf16[320,2048]{1,0:T(8,128)(2,1)S(1)}, bf16[320,2048]{1,0:T(8,128)(2,1)S(1)}, u32[]{:S(2)}, u32[]{:S(2)}) collective-permute-start(bf16[320,2048]{1,0:T(8,128)(2,1)S(1)} %pack.5.refs_0_), channel_id=1, source_target_pairs={{0,1},{1,0},{2,3},{3,2},{4,5},{5,4},{6,7},{7,6},{8,9},{9,8},{10,11... | collective-permute-start | bytes 3932168 | tf_op jit(solution)/shard_map/ppermute | solution.py:26
  59.2 30.8 %collective-permute-start.11 = (bf16[320,2048]{1,0:T(8,128)(2,1)S(1)}, bf16[320,2048]{1,0:T(8,128)(2,1)}, u32[]{:S(2)}, u32[]{:S(2)}) collective-permute-start(bf16[320,2048]{1,0:T(8,128)(2,1)S(1)} %pack.5.refs_0_), channel_id=1, source_target_pairs={{0,2},{1,3},{2,0},{3,1},{4,6},{5,7},{6,4},{7,5},{8,10},{9,11},{10,... | collective-permute-start | bytes 3932168 | tf_op jit(solution)/shard_map/ppermute | solution.py:26
  61.4 16.9 %copy-start.8 = (f32[160,128]{1,0:T(8,128)}, f32[160,128]{1,0:T(8,128)S(1)}, u32[]{:S(2)}) copy-start(f32[160,128]{1,0:T(8,128)S(1)} %get-tuple-element.264.refs_13_) | copy-start | bytes 245764
  90.0 5.1 %collective-permute-start.14 = (bf16[320,2048]{1,0:T(8,128)(2,1)}, bf16[320,2048]{1,0:T(8,128)(2,1)S(1)}, u32[]{:S(2)}, u32[]{:S(2)}) collective-permute-start(bf16[320,2048]{1,0:T(8,128)(2,1)} %collective-permute-done.11.refs_0_), channel_id=1, source_target_pairs={{0,1},{1,0},{2,3},{3,2},{4,5},{5,4},{6,7},{7,6},{8,9},{9,8},{10,11... | collective-permute-start | bytes 3932168 | tf_op jit(solution)/shard_map/ppermute | solution.py:26
  103.2 13.1 %copy-start.14 = (f32[8,160]{1,0:T(8,128)S(1)}, f32[8,160]{1,0:T(8,128)}, u32[]{:S(2)}) copy-start(f32[8,160]{1,0:T(8,128)} %param.17) | copy-start | bytes 15364
  103.2 6.0 %collective-permute-start.15 = (f32[2,160]{1,0:T(2,128)S(1)}, f32[2,160]{1,0:T(2,128)S(1)}, u32[]{:S(2)}, u32[]{:S(2)}) collective-permute-start(f32[2,160]{1,0:T(2,128)S(1)} %get-tuple-element.250), channel_id=1, source_target_pairs={{0,4},{4,0},{8,12},{12,8},{16,20},{20,16},{24,28},{28,24},{1,5},{5... | collective-permute-start | bytes 3848 | tf_op jit(solution)/shard_map/ppermute | solution.py:26
  105.0 4.2 %collective-permute-start.17 = (f32[1,160]{1,0:T(1,128)S(1)}, f32[1,160]{1,0:T(1,128)S(1)}, u32[]{:S(2)}, u32[]{:S(2)}) collective-permute-start(f32[1,160]{1,0:T(1,128)S(1)} %get-tuple-element.252), channel_id=1, source_target_pairs={{0,8},{4,12},{8,0},{12,4},{16,24},{20,28},{24,16},{28,20},{1,9},{5... | collective-permute-start | bytes 1928 | tf_op jit(solution)/shard_map/ppermute | solution.py:26
  106.6 4.5 %collective-permute-start.16 = (f32[1,160]{1,0:T(1,128)S(1)}, f32[1,160]{1,0:T(1,128)S(1)}, u32[]{:S(2)}, u32[]{:S(2)}) collective-permute-start(f32[1,160]{1,0:T(1,128)S(1)} %get-tuple-element.251), channel_id=1, source_target_pairs={{0,16},{4,20},{8,24},{12,28},{16,0},{20,4},{24,8},{28,12},{1,17},{... | collective-permute-start | bytes 1928 | tf_op jit(solution)/shard_map/ppermute | solution.py:26
  111.2 1.2 %collective-permute-start.18 = (f32[8,160]{1,0:T(8,128)S(1)}, f32[8,160]{1,0:T(8,128)S(1)}, u32[]{:S(2)}, u32[]{:S(2)}) collective-permute-start(f32[8,160]{1,0:T(8,128)S(1)} %select_select_fusion), channel_id=1, source_target_pairs={{0,1},{1,0},{2,3},{3,2},{4,5},{5,4},{6,7},{7,6},{8,9},{9,8},{10,11... | collective-permute-start | bytes 15368 | tf_op jit(solution)/shard_map/ppermute | solution.py:26
  112.4 3.7 %collective-permute-start.19 = (f32[8,160]{1,0:T(8,128)S(1)}, f32[8,160]{1,0:T(8,128)S(1)}, u32[]{:S(2)}, u32[]{:S(2)}) collective-permute-start(f32[8,160]{1,0:T(8,128)S(1)} %fusion.29), channel_id=1, source_target_pairs={{0,2},{1,3},{2,0},{3,1},{4,6},{5,7},{6,4},{7,5},{8,10},{9,11},{10,... | collective-permute-start | bytes 15368 | tf_op jit(solution)/shard_map/ppermute | solution.py:26
  116.1 0.9 copy-start.13

commit v2 on v1

--- a/solution.py
+++ b/solution.py
@@ -15,6 +15,7 @@
 ROPE_BASE = 500000.0
 DEPTH = 1024
 PARTS = 4
+STAGED = (2, 3)
 GRAIN = 16
 ROUTES = (1, 2, 4, 1)
 BITS = (1, 2, 4)
@@ -33,14 +34,19 @@
     return total
 
 
-def add_products(x, gain_ref, wq_ref, wk_ref, wv_ref, q_acc, kv_acc, ss_acc, wkv):
-    wkv[:, :HD] = wk_ref[...]
-    wkv[:, HD:] = wv_ref[...]
+def add_products(x, gain_ref, w_refs, q_acc, kv_acc, ss_acc, wkv):
+    if len(w_refs) == 1:
+        width = q_acc.shape[1]
+        wq, w_rest = w_refs[0][:, :width], w_refs[0][:, width:]
+    else:
+        wkv[:, :HD] = w_refs[1][...]
+        wkv[:, HD:] = w_refs[2][...]
+        wq, w_rest = w_refs[0][...], wkv[...]
     xf = x.astype(jnp.float32)
     ss_acc[...] += lane_groups(xf * xf)
     scaled = (xf * gain_ref[...]).astype(jnp.bfloat16)
-    q_acc[...] += jnp.dot(scaled, wq_ref[...], preferred_element_type=jnp.float32)
-    kv_acc[...] += jnp.dot(scaled, wkv[...], preferred_element_type=jnp.float32)
+    q_acc[...] += jnp.dot(scaled, wq, preferred_element_type=jnp.float32)
+    kv_acc[...] += jnp.dot(scaled, w_rest, preferred_element_type=jnp.float32)
 
 
 def by_part(step, blocks, x_refs, act):
@@ -51,11 +57,12 @@
             act(f, refs)
 
 
-def sums_kernel(parts, groups, begun, part_ref, *refs):
+def sums_kernel(parts, arrays, groups, begun, part_ref, *refs):
     refs = list(refs)
     take = lambda n: [refs.pop(0) for _ in range(n)]
     x_refs = [take(groups) for _ in range(parts)]
-    weights = take(4)
+    (gain_ref,) = take(1)
+    weights = take(arrays)
     (head_ref,) = take(1)
     begun_refs = [take(4) for _ in range(groups)] if begun else None
     outs = [take(4) for _ in range(groups)]
@@ -73,7 +80,7 @@
             x = x_ref[...]
             if f == 0 and not begun:
                 vt_ref[...] += lane_groups(x.astype(jnp.float32) * head_ref[...])
-            add_products(x, *weights, q_ref, kv_ref, ss_ref, wkv)
+            add_products(x, gain_ref, weights, q_ref, kv_ref, ss_ref, wkv)
 
     by_part(step, pl.num_programs(0) // parts, x_refs, act)
 
@@ -82,11 +89,11 @@
     return (value * cosine + pltpu.roll(value, HD // 2, 1) * sine).astype(jnp.bfloat16)
 
 
-def attend_kernel(slot, tile, begin, parts, last, part_ref, place_ref, *refs):
+def attend_kernel(slot, tile, begin, parts, arrays, last, part_ref, place_ref, *refs):
     if last:
         info_ref, refs = refs[0], refs[1:]
     x_refs, refs = [[ref] for ref in refs[:parts]], refs[parts:]
-    weights, refs = refs[:4], refs[4:]
+    gain_ref, weights, refs = refs[0], refs[1 : 1 + arrays], refs[1 + arrays :]
     if last:
         (total_ref, line_ref, *back_refs, rows_ref), refs = refs[-3 - len(BITS) :], refs[: -3 - len(BITS)]
     (
@@ -121,7 +128,7 @@
         lax.fori_loop(0, rows // GRAIN, place, 0)
 
     def act(f, rows):
-        add_products(rows[0][...], *weights, q_acc, kv_acc, ss_acc, wkv)
+        add_products(rows[0][...], gain_ref, weights, q_acc, kv_acc, ss_acc, wkv)
 
     by_part(step, steps // parts, x_refs, act)
 
@@ -368,9 +375,36 @@
             flip = jnp.where(step < f * blocks, flip, flips[f])
         return (part_ref[0] ^ flip) * blocks + lax.rem(step, blocks)
 
+    def staged_row(step, *rest):
+        return (flips[0] - STAGED[0]) * blocks + step
+
+    held = row if len(widths) > 1 else staged_row
     return [pl.BlockSpec((1, DEPTH), lambda k, *p: (0, row(k, *p)))] + [
-        pl.BlockSpec((DEPTH, width), lambda k, *p: (row(k, *p), 0)) for width in widths
+        pl.BlockSpec((DEPTH, width), lambda k, *p: (held(k, *p), 0)) for width in widths
     ]
+
+
+def stage_kernel(part_ref, *refs):
+    weights, (out_ref, sems) = refs[:-2], refs[-2:]
+    height = out_ref.shape[0] // len(STAGED)
+    copies = []
+    for f, flip in enumerate(STAGED):
+        at = 0
+        for i, w_ref in enumerate(weights):
+            width = w_ref.shape[1]
+            begin = pl.multiple_of((part_ref[0] ^ flip) * height, height)
+            copies.append(
+                pltpu.make_async_copy(
+                    w_ref.at[pl.ds(begin, height)],
+                    out_ref.at[pl.ds(f * height, height), pl.ds(at, width)],
+                    sems.at[f * len(weights) + i],
+                )
+            )
+            at += width
+    for copy in copies:
+        copy.start()
+    for copy in copies:
+        copy.wait()
 
 
 def x_spec(rows, blocks, f):
@@ -395,10 +429,11 @@
     groups = len(xs[0])
     blocks = xs[0][0].shape[1] // DEPTH
     counts = [x.shape[0] for x in xs[0]]
-    outs = [(count, width) for count in counts for width in (widths[0], sum(widths[1:]), HD, HD)]
+    columns = sum(widths)
+    outs = [(count, width) for count in counts for width in (columns - 2 * HD, 2 * HD, HD, HD)]
     given = [a for group in begun for a in group] if begun else []
     sums = pl.pallas_call(
-        functools.partial(sums_kernel, len(flips), groups, begun is not None),
+        functools.partial(sums_kernel, len(flips), len(weights), groups, begun is not None),
         grid_spec=pltpu.PrefetchScalarGridSpec(
             num_scalar_prefetch=1,
             grid=(len(flips) * blocks,),
@@ -423,7 +458,8 @@
     count, blocks = xs[0].shape[0], xs[0].shape[1] // DEPTH
     slot = tables[0].shape[0]
     tile = max(t for t in range(GRAIN, 97, GRAIN) if count % t == 0)
-    stacked = widths[0] // HD * tile
+    q_width = sum(widths) - 2 * HD
+    stacked = q_width // HD * tile
     scalars, given, lines, space = [part, places], [], [], []
     if last:
         info, ahead, rollouts, rows = last
@@ -436,13 +472,13 @@
     ]
 
     def kernel(*refs):
-        n = len(scalars) + len(flips) + 4 + len(sums) + len(tables) + len(before)
+        n = len(scalars) + len(flips) + 1 + len(weights) + len(sums) + len(tables) + len(before)
         inputs, more, refs = refs[:n], refs[n : n + len(given)], refs[n + len(given) :]
         own, rest = refs[: len(outs)], refs[len(outs) :]
         extra, scratch = rest[: len(lines)], rest[len(lines) :]
         scratch, room = scratch[: len(scratch) - len(space)], scratch[len(scratch) - len(space) :]
         attend_kernel(
-            slot, tile, begin, len(flips), last is not None,
+            slot, tile, begin, len(flips), len(weights), last is not None,
             *inputs, *own, *scratch, *more, *extra, *room,
         )
 
@@ -456,8 +492,8 @@
             + [fixed(*a.shape) for a in (*sums, *tables, *before, *given)],
             out_specs=[fixed(*a.shape) for a in (*outs, *lines)],
             scratch_shapes=[
-                pltpu.VMEM((count, widths[0]), jnp.float32),
-                pltpu.VMEM((count, widths[1] + widths[2]), jnp.float32),
+                pltpu.VMEM((count, q_width), jnp.float32),
+                pltpu.VMEM((count, 2 * HD), jnp.float32),
                 pltpu.VMEM((count, HD), jnp.float32),
                 pltpu.VMEM((count, HD), jnp.float32),
                 pltpu.VMEM((count, HD), jnp.float32),
@@ -591,12 +627,25 @@
     total_first, *before = attend(0, places_first, far_first, sums_first, before)
     x_second, near_second, _ = lax.optimization_barrier((x_second, near_second, total_first))
     (sums_second,) = sums_call(shared, (0, 1), [[x_second], [near_second]], head)
-    far_second, sums_second = lax.optimization_barrier((far_second, sums_second))
+    part_then, sums_second = lax.optimization_barrier((part, sums_second))
+    staged = pl.pallas_call(
+        stage_kernel,
+        in_specs=[scalars] + [anywhere] * len(weights),
+        out_specs=onchip,
+        out_shape=whole(
+            (len(STAGED) * part_width, sum(w.shape[1] for w in weights)), w_query.dtype
+        ),
+        scratch_shapes=[pltpu.SemaphoreType.DMA((len(STAGED) * len(weights),))],
+        compiler_params=pltpu.CompilerParams(vmem_limit_bytes=24 << 20),
+        name="stage",
+    )(part_then, *weights)
+    far_second, sums_second, staged = lax.optimization_barrier((far_second, sums_second, staged))
+    held = (part, gain, (staged,))
     far_near = swapped(far_second, "mp", 1)
-    (sums_second,) = sums_call(shared, (2,), [[far_second]], head, begun=[sums_second])
+    (sums_second,) = sums_call(held, (2,), [[far_second]], head, begun=[sums_second])
     far_near, sums_second = lax.optimization_barrier((far_near, sums_second))
     total_second, key_rows, val_rows, *lines = attend_call(
-        shared, tables, first, places, (3,), [far_near], sums_second, before,
+        held, tables, first, places, (3,), [far_near], sums_second, before,
         last=(info, total_first, rollouts, rows),
     )
 

time: 117 us -> 119 us (1.017)
  local copies, waits for them, and re-layouts: 1.54 us -> 9.54 us
  Pallas kernels: 55.9 us -> 52.5 us
  waiting for transfers between devices: 29.4 us -> 26.4 us
    unnamed x28 -> x36, local copies, waits for them, and re-layouts: 0.71 us -> 8.71 us
    ppermute x14, waiting for transfers between devices: 29.4 us -> 26.4 us  [swapped(): return lax.ppermute(value, axis, [(i, i ^ bit) for i in range(length)])]
    pallas_call x2, Pallas kernels: 23.1 us -> 21 us  [attend_call(): pl.pallas_call(kernel, grid_spec=pltpu.PrefetchScalarGridSpec(num_scalar_...]
    pallas_call x3 -> x4, Pallas kernels: 22.5 us -> 21.9 us  [the longest x3 20.2 us: sums_call(): pl.pallas_call(functools.partial(sums_kernel, len(flips), len(weights), g...]
  transfers between devices with their start and end apart: 14 -> 14, of which waited for: 8 -> 8; matrix products, arithmetic and copies ran while one was open for 1% -> 1% of each run, Pallas kernels for 38% -> 35%
where the time goes in v2:
time: 119 us
  Pallas kernels  52.5 us (44%)
  waiting for transfers between devices  26.4 us (22%)
  starting transfers between devices  15.6 us (13%)
  blocking collectives  11.6 us (10%)
  local copies, waits for them, and re-layouts  9.54 us (8%)
  between operations  1.6 us (1%)
    ppermute x14, waiting for transfers between devices, swapped(): return lax.ppermute(value, axis, [(i, i ^ bit) for i in range(length)])  26.4 us
    pallas_call x2, Pallas kernels, attend_call(): pl.pallas_call(kernel, grid_spec=pltpu.PrefetchScalarGridSpec(num_scalar_...  21 us
    pallas_call x3, Pallas kernels, sums_call(): pl.pallas_call(functools.partial(sums_kernel, len(flips), len(weights), g...  20.2 us
    ppermute x14, starting transfers between devices, swapped(): return lax.ppermute(value, axis, [(i, i ^ bit) for i in range(length)])  15.6 us
    psum x1, blocking collectives, local(): lax.psum(jnp.where(jnp.arange(owners)[:, None] == me, lengths[None, :], 0...  11.6 us
    unnamed x36, local copies, waits for them, and re-layouts  8.71 us
    pallas_call x1, Pallas kernels, local(): pl.pallas_call(functools.partial(plan_kernel, slot_blocks, first // GRAIN...  3.98 us
    pallas_call x1, Pallas kernels, local(): pl.pallas_call(functools.partial(first_pack_kernel, slot_blocks), in_spec...  3.6 us
  transfers between devices with their start and end apart: 14, of which 8 were waited for; matrix products, arithmetic and copies ran while one was open for 1% of the time, Pallas kernels for 35%

profile of v2, /device:TPU:0, one launch (start us, length us, event | category | flops | bytes accessed | tf_op | source)
XLA Modules:
  0.0 119.0 jit_solution(11782883386802627489)
XLA Ops:
  0.6 0.6 copy-done.4
  1.3 3.6 %first_pack.1 = (s32[35]{0:T(128)S(1)}, bf16[560,2048]{1,0:T(8,128)(2,1)}) custom-call(s32[8]{0:T(128)S(1)} %copy-done.4, bf16[1280,2048]{1,0:T(8,128)(2,1)} %hidden_ref.5), custom_call_target="tpu_custom_call" | custom-call | tf_op jit(solution)/shard_map/first_pack/pallas_call | solution.py:561
  4.9 0.5 collective-permute-start.6
  5.4 2.6 %collective-permute-start.10 = (bf16[560,2048]{1,0:T(8,128)(2,1)}, bf16[560,2048]{1,0:T(8,128)(2,1)S(1)}, u32[]{:S(2)}, u32[]{:S(2)}) collective-permute-start(bf16[560,2048]{1,0:T(8,128)(2,1)} %get-tuple-element.204.refs_0_), channel_id=1, source_target_pairs={{0,2},{1,3},{2,0},{3,1},{4,6},{5,7},{6,4},{7,5},{8,10},{9,11},{10,... | collective-permute-start | bytes 6881288 | tf_op jit(solution)/shard_map/ppermute | solution.py:27
  8.0 0.1 broadcast_select_fusion
  8.1 0.1 reshape.34
  8.2 11.6 %psum.7.lengths_ref = s32[64]{0:T(128)S(1)} all-reduce(s32[64]{0:T(128)S(1)} %reshape.34), channel_id=1, replica_groups=mesh['dp'=8,'mp'=4] {'dp'}, use_global_device_ids=true, to_apply=%region_0.1 | all-reduce | flops 64 | bytes 512 | tf_op jit(solution)/shard_map/psum | solution.py:575
  19.8 4.0 %plan.1 = (s32[80]{0:T(128)S(1)}, s32[80]{0:T(128)S(1)}, s32[64]{0:T(128)S(1)}, bf16[320,2048]{1,0:T(8,128)(2,1)}, bf16[160,2048]{1,0:T(8,128)(2,1)}, /*index=5*/bf16[160,2048]{1,0:T(8,128)(2,1)S(1)}) custom-call(s32[1]{0:T(128)} %bitcast.me_ref, s32[64]{0:T(128)S(1)} %psum.7.lengths_ref, bf16[1280,2048]{1,0:T(8,128)(2,1)} %hidden_ref.5), custom_call_target="tpu_custom_call" | custom-call | tf_op jit(solution)/shard_map/plan/pallas_call | solution.py:578
  23.8 1.9 %collective-permute-start.7 = (bf16[320,2048]{1,0:T(8,128)(2,1)}, bf16[320,2048]{1,0:T(8,128)(2,1)}, u32[]{:S(2)}, u32[]{:S(2)}) collective-permute-start(bf16[320,2048]{1,0:T(8,128)(2,1)} %get-tuple-element.209), channel_id=1, source_target_pairs={{0,4},{4,0},{8,12},{12,8},{16,20},{20,16},{24,28},{28,24},{1,5},{5... | collective-permute-start | bytes 3932168 | tf_op jit(solution)/shard_map/ppermute | solution.py:27
  25.7 0.2 collective-permute-start.8
  25.9 0.2 collective-permute-start.9
  26.1 0.1 slice.31
  26.2 0.1 slice_compare_fusion
  26.3 0.1 fusion.24
  26.4 0.6 slice.32
  27.0 0.0 slice-start
  27.0 11.8 %sums.7 = (f32[560,1024]{1,0:T(8,128)S(1)}, f32[560,256]{1,0:T(8,128)S(1)}, f32[560,128]{1,0:T(8,128)S(1)}, f32[560,128]{1,0:T(8,128)S(1)}) custom-call(s32[1]{0:T(128)} %bitcast.2.part_ref.refs_0_, bf16[560,2048]{1,0:T(8,128)(2,1)} %get-tuple-element.204.refs_0_, bf16[560,2048]{1,0:T(8,128)(2,1)} %collective-permute-done.6.refs_1_, f32[1,8192]{1,0:T(1,128)S(1)} %bitcast.24, ...), custom_call_target="tpu_custom_call" | custom-call | flops 5872025600 | bytes 17940480 | tf_op jit(solution)/shard_map/sums/pallas_call | solution.py:435
  38.8 14.3 %collective-permute-done.8.refs_1_ = bf16[160,2048]{1,0:T(8,128)(2,1)} collective-permute-done((bf16[160,2048]{1,0:T(8,128)(2,1)}, bf16[160,2048]{1,0:T(8,128)(2,1)}, u32[]{:S(2)}, u32[]{:S(2)}) %collective-permute-start.8) | collective-permute-done | bytes 655392 | tf_op jit(solution)/shard_map/ppermute | solution.py:27
  53.0 2.0 %collective-permute-done.9.refs_2_ = bf16[160,2048]{1,0:T(8,128)(2,1)} collective-permute-done((bf16[160,2048]{1,0:T(8,128)(2,1)S(1)}, bf16[160,2048]{1,0:T(8,128)(2,1)}, u32[]{:S(2)}, u32[]{:S(2)}) %collective-permute-start.9) | collective-permute-done | bytes 655392 | tf_op jit(solution)/shard_map/ppermute | solution.py:27
  55.1 0.0 slice-start.3
  55.1 2.1 %pack.5.refs_0_ = bf16[320,2048]{1,0:T(8,128)(2,1)S(1)} custom-call(s32[80]{0:T(128)S(1)} %get-tuple-element.215.source_ref, bf16[1280,2048]{1,0:T(8,128)(2,1)S(1)} %bitcast.23, bf16[320,2048]{1,0:T(8,128)(2,1)} %collective-permute-done.7.refs_0_, bf16[160,2048]{1,0:T(8,128)(2,1)} %collective-permute-done.8.refs_1_, ...), custom_call_target="tpu_custom_call" | custom-call | tf_op jit(solution)/shard_map/pack/pallas_call | solution.py:602
  57.2 1.4 %collective-permute-done.10.refs_2_ = bf16[560,2048]{1,0:T(8,128)(2,1)S(1)} collective-permute-done((bf16[560,2048]{1,0:T(8,128)(2,1)}, bf16[560,2048]{1,0:T(8,128)(2,1)S(1)}, u32[]{:S(2)}, u32[]{:S(2)}) %collective-permute-start.10) | collective-permute-done | bytes 2293792 | tf_op jit(solution)/shard_map/ppermute | solution.py:27
  58.7 0.5 collective-permute-start.12
  59.2 1.8 %collective-permute-start.11 = (bf16[320,2048]{1,0:T(8,128)(2,1)S(1)}, bf16[320,2048]{1,0:T(8,128)(2,1)}, u32[]{:S(2)}, u32[]{:S(2)}) collective-permute-start(bf16[320,2048]{1,0:T(8,128)(2,1)S(1)} %pack.5.refs_0_), channel_id=1, source_target_pairs={{0,2},{1,3},{2,0},{3,1},{4,6},{5,7},{6,4},{7,5},{8,10},{9,11},{10,... | collective-permute-start | bytes 3932168 | tf_op jit(solution)/shard_map/ppermute | solution.py:27
  60.9 0.3 fusion.12
  61.3 0.1 pad_maximum_fusion
  61.4 1.7 %collective-permute-done.13.refs_3_ = bf16[560,2048]{1,0:T(8,128)(2,1)S(1)} collective-permute-done((bf16[560,2048]{1,0:T(8,128)(2,1)S(1)}, bf16[560,2048]{1,0:T(8,128)(2,1)S(1)}, u32[]{:S(2)}, u32[]{:S(2)}) %collective-permute-start.13) | collective-permute-done | bytes 2293792 | tf_op jit(solution)/shard_map/ppermute | solution.py:27
  63.2 13.9 %attend.6 = (f32[560,128]{1,0:T(8,128)}, bf16[160,128]{1,0:T(8,128)(2,1)S(1)}, bf16[160,128]{1,0:T(8,128)(2,1)S(1)}) custom-call(s32[1]{0:T(128)} %bitcast.2.part_ref.refs_0_, s32[35]{0:T(128)S(1)} %get-tuple-element.220.refs_1_, bf16[560,2048]{1,0:T(8,128)(2,1)S(1)} %collective-permute-done.10.refs_2_, ...), custom_call_target="tpu_custom_call" | custom-call | flops 5872025600 | bytes 17940480 | tf_op jit(solution)/shard_map/attend/pallas_call | solution.py:485
  77.1 5.0 %sums.8 = (f32[320,1024]{1,0:T(8,128)S(1)}, f32[320,256]{1,0:T(8,128)S(1)}, f32[320,128]{1,0:T(8,128)S(1)}, f32[320,128]{1,0:T(8,128)S(1)}) custom-call(s32[1]{0:T(128)} %bitcast.2.part_ref.refs_0_, bf16[320,2048]{1,0:T(8,128)(2,1)S(1)} %pack.5.refs_0_, bf16[320,2048]{1,0:T(8,128)(2,1)S(1)} %collective-permute-done.12.refs_1_, f32[1,8192]{1,0:T(1,128)S(1)} %bitcast.26, ...), custom_call_target="tpu_custom_call" | custom-call | flops 3355443200 | bytes 14745600 | tf_op jit(solution)/shard_map/sums/pallas_call | solution.py:435
  82.1 1.7 %stage.1.refs_2_.refs_5_ = bf16[4096,1280]{1,0:T(8,128)(2,1)S(1)} custom-call(s32[1]{0:T(128)} %bitcast.2.part_ref.refs_0_, bf16[8192,1024]{1,0:T(8,128)(2,1)S(1)} %bitcast.19, bf16[8192,128]{1,0:T(8,128)(2,1)S(1)} %copy-done.7, bf16[8192,128]{1,0:T(8,128)(2,1)S(1)} %copy-done.10), custom_call_target="tpu_custom_call" | custom-call | tf_op jit(solution)/shard_map/stage/pallas_call | solution.py:631
  83.8 4.0 %copy-done = bf16[4096,1280]{1,0:T(8,128)(2,1)} copy-done((bf16[4096,1280]{1,0:T(8,128)(2,1)}, bf16[4096,1280]{1,0:T(8,128)(2,1)S(1)}, u32[]{:S(2)}) %copy-start) | copy-done | bytes 10485784
  87.9 2.1 %collective-permute-done.11.refs_0_ = bf16[320,2048]{1,0:T(8,128)(2,1)} collective-permute-done((bf16[320,2048]{1,0:T(8,128)(2,1)S(1)}, bf16[320,2048]{1,0:T(8,128)(2,1)}, u32[]{:S(2)}, u32[]{:S(2)}) %collective-permute-start.11) | collective-permute-done | bytes 1310752 | tf_op jit(solution)/shard_map/ppermute | solution.py:27
  90.6 4.0 %copy-done.1 = bf16[4096,1280]{1,0:T(8,128)(2,1)S(1)} copy-done((bf16[4096,1280]{1,0:T(8,128)(2,1)S(1)}, bf16[4096,1280]{1,0:T(8,128)(2,1)}, u32[]{:S(2)}) %copy-start.1) | copy-done | bytes 10485784
  94.6 3.3 %sums.9 = (f32[320,1024]{1,0:T(8,128)S(1)}, f32[320,256]{1,0:T(8,128)S(1)}, f32[320,128]{1,0:T(8,128)S(1)}, f32[320,128]{1,0:T(8,128)S(1)}) custom-call(s32[1]{0:T(128)} %bitcast.2.part_ref.refs_0_, bf16[320,2048]{1,0:T(8,128)(2,1)} %collective-permute-done.11.refs_0_, f32[1,8192]{1,0:T(1,128)S(1)} %bitcast.27, bf16[4096,1280]{1,0:T(8,128)(2,1)S(1)} %copy-done.1, ...), custom_call_target="tpu_custom_call" | custom-call | flops 1677721600 | bytes 8192000 | tf_op jit(solution)/shard_map/sums/pallas_call | solution.py:435
  98.0 7.1 %attend.7 = (f32[320,128]{1,0:T(8,128)S(1)}, bf16[160,128]{1,0:T(8,128)(2,1)S(1)}, bf16[160,128]{1,0:T(8,128)(2,1)S(1)}, f32[8,160]{1,0:T(8,128)S(1)}, f32[2,160...) custom-call(s32[1]{0:T(128)} %bitcast.2.part_ref.refs_0_, s32[80]{0:T(128)S(1)} %get-tuple-element.214.refs_1_, ...), custom_call_target="tpu_custom_call" | custom-call | flops 1677721600 | bytes 8192000 | tf_op jit(solution)/shard_map/attend/pallas_call | solution.py:485
  105.1 1.8 %collective-permute-start.15 = (f32[2,160]{1,0:T(2,128)S(1)}, f32[2,160]{1,0:T(2,128)S(1)}, u32[]{:S(2)}, u32[]{:S(2)}) collective-permute-start(f32[2,160]{1,0:T(2,128)S(1)} %get-tuple-element.262), channel_id=1, source_target_pairs={{0,4},{4,0},{8,12},{12,8},{16,20},{20,16},{24,28},{28,24},{1,5},{5... | collective-permute-start | bytes 3848 | tf_op jit(solution)/shard_map/ppermute | solution.py:27
  106.9 1.6 %collective-permute-start.17 = (f32[1,160]{1,0:T(1,128)S(1)}, f32[1,160]{1,0:T(1,128)S(1)}, u32[]{:S(2)}, u32[]{:S(2)}) collective-permute-start(f32[1,160]{1,0:T(1,128)S(1)} %get-tuple-element.264), channel_id=1, source_target_pairs={{0,8},{4,12},{8,0},{12,4},{16,24},{20,28},{24,16},{28,20},{1,9},{5... | collective-permute-start | bytes 1928 | tf_op jit(solution)/shard_map/ppermute | solution.py:27
  108.5 2.9 %collective-permute-start.16 = (f32[1,160]{1,0:T(1,128)S(1)}, f32[1,160]{1,0:T(1,128)S(1)}, u32[]{:S(2)}, u32[]{:S(2)}) collective-permute-start(f32[1,160]{1,0:T(1,128)S(1)} %get-tuple-element.263), channel_id=1, source_target_pairs={{0,16},{4,20},{8,24},{12,28},{16,0},{20,4},{24,8},{28,12},{1,17},{... | collective-permute-start | bytes 1928 | tf_op jit(solution)/shard_map/ppermute | solution.py:27
  111.4 1.6 %collective-permute-done.16 = f32[1,160]{1,0:T(1,128)S(1)} collective-permute-done((f32[1,160]{1,0:T(1,128)S(1)}, f32[1,160]{1,0:T(1,128)S(1)}, u32[]{:S(2)}, u32[]{:S(2)}) %collective-permute-start.16) | collective-permute-done | bytes 672 | tf_op jit(solution)/shard_map/ppermute | solution.py:27
  113.0 0.1 select_select_fusion
  113.1 0.0 collective-permute-start.18
  113.1 1.2 collective-permute-done.18
  114.3 0.1 fusion.29
  114.3 1.5 %collective-permute-start.19 = (f32[8,160]{1,0:T(8,128)S(1)}, f32[8,160]{1,0:T(8,128)S(1)}, u32[]{:S(2)}, u32[]{:S(2)}) collective-permute-start(f32[8,160]{1,0:T(8,128)S(1)} %fusion.29), channel_id=1, source_target_pairs={{0,2},{1,3},{2,0},{3,1},{4,6},{5,7},{6,4},{7,5},{8,10},{9,11},{10,... | collective-permute-start | bytes 15368 | tf_op jit(solution)/shard_map/ppermute | solution.py:27
  115.9 2.1 %collective-permute-done.19 = f32[8,160]{1,0:T(8,128)S(1)} collective-permute-done((f32[8,160]{1,0:T(8,128)S(1)}, f32[8,160]{1,0:T(8,128)S(1)}, u32[]{:S(2)}, u32[]{:S(2)}) %collective-permute-start.19) | collective-permute-done | bytes 5152 | tf_op jit(solution)/shard_map/ppermute | solution.py:27
  118.0 0.1 add_select_fusion
  118.1 0.1 slice.42
  118.1 0.8 fusion
  (48 shorter events, 0.1 us)
Async XLA Ops:
  0.6 0.7 copy-start.4
  1.3 6.7 %copy-start.5 = (s32[8]{0:T(128)S(1)}, s32[8]{0:T(128)}, u32[]{:S(2)}) copy-start(s32[8]{0:T(128)} %lengths_ref.1) | copy-start | bytes 100
  4.9 22.0 %collective-permute-start.6 = (bf16[560,2048]{1,0:T(8,128)(2,1)}, bf16[560,2048]{1,0:T(8,128)(2,1)}, u32[]{:S(2)}, u32[]{:S(2)}) collective-permute-start(bf16[560,2048]{1,0:T(8,128)(2,1)} %get-tuple-element.204.refs_0_), channel_id=1, source_target_pairs={{0,1},{1,0},{2,3},{3,2},{4,5},{5,4},{6,7},{7,6},{8,9},{9,8},{10,11... | collective-permute-start | bytes 6881288 | tf_op jit(solution)/shard_map/ppermute | solution.py:27
  5.4 53.2 %collective-permute-start.10 = (bf16[560,2048]{1,0:T(8,128)(2,1)}, bf16[560,2048]{1,0:T(8,128)(2,1)S(1)}, u32[]{:S(2)}, u32[]{:S(2)}) collective-permute-start(bf16[560,2048]{1,0:T(8,128)(2,1)} %get-tuple-element.204.refs_0_), channel_id=1, source_target_pairs={{0,2},{1,3},{2,0},{3,1},{4,6},{5,7},{6,4},{7,5},{8,10},{9,11},{10,... | collective-permute-start | bytes 6881288 | tf_op jit(solution)/shard_map/ppermute | solution.py:27
  19.8 7.2 %copy-start.13 = (f32[8192]{0:T(1024)S(1)}, f32[8192]{0:T(1024)}, u32[]{:S(2)}) copy-start(f32[8192]{0:T(1024)} %param.19) | copy-start | bytes 98308
  19.8 7.2 %copy-start.19 = (f32[2048]{0:T(1024)S(1)}, f32[2048]{0:T(1024)}, u32[]{:S(2)}) copy-start(f32[2048]{0:T(1024)} %param.23) | copy-start | bytes 24580
  23.8 31.3 %collective-permute-start.7 = (bf16[320,2048]{1,0:T(8,128)(2,1)}, bf16[320,2048]{1,0:T(8,128)(2,1)}, u32[]{:S(2)}, u32[]{:S(2)}) collective-permute-start(bf16[320,2048]{1,0:T(8,128)(2,1)} %get-tuple-element.209), channel_id=1, source_target_pairs={{0,4},{4,0},{8,12},{12,8},{16,20},{20,16},{24,28},{28,24},{1,5},{5... | collective-permute-start | bytes 3932168 | tf_op jit(solution)/shard_map/ppermute | solution.py:27
  25.7 27.3 %collective-permute-start.8 = (bf16[160,2048]{1,0:T(8,128)(2,1)}, bf16[160,2048]{1,0:T(8,128)(2,1)}, u32[]{:S(2)}, u32[]{:S(2)}) collective-permute-start(bf16[160,2048]{1,0:T(8,128)(2,1)} %get-tuple-element.210), channel_id=1, source_target_pairs={{0,8},{4,12},{8,0},{12,4},{16,24},{20,28},{24,16},{28,20},{1,9},{5... | collective-permute-start | bytes 1966088 | tf_op jit(solution)/shard_map/ppermute | solution.py:27
  25.9 29.1 %collective-permute-start.9 = (bf16[160,2048]{1,0:T(8,128)(2,1)S(1)}, bf16[160,2048]{1,0:T(8,128)(2,1)}, u32[]{:S(2)}, u32[]{:S(2)}) collective-permute-start(bf16[160,2048]{1,0:T(8,128)(2,1)S(1)} %get-tuple-element.211), channel_id=1, source_target_pairs={{0,16},{4,20},{8,24},{12,28},{16,0},{20,4},{24,8},{28,12},{1,17},{... | collective-permute-start | bytes 1966088 | tf_op jit(solution)/shard_map/ppermute | solution.py:27
  26.9 28.1 %slice-start.8 = ((s8[5242880]{0:T(1024)(128)(4,1)}), s8[4194304]{0:T(1024)(128)(4,1)S(1)}, s32[]{:S(2)}) async-start(s8[5242880]{0:T(1024)(128)(4,1)} %bitcast.22), calls=%async_computation.8 | async-start | bytes 8388608
  26.9 28.1 %slice-start.9 = ((s8[5242880]{0:T(1024)(128)(4,1)}), s8[1048576]{0:T(1024)(128)(4,1)S(1)}, s32[]{:S(2)}) async-start(s8[5242880]{0:T(1024)(128)(4,1)} %bitcast.22), calls=%async_computation.9 | async-start | bytes 2097152
  27.0 36.2 %slice-start = ((s8[16777216]{0:T(1024)(128)(4,1)}), s8[4194304]{0:T(1024)(128)(4,1)S(1)}, s32[]{:S(2)}) async-start(s8[16777216]{0:T(1024)(128)(4,1)} %bitcast.18), calls=%async_computation | async-start | bytes 8388608
  27.0 36.1 %slice-start.1 = ((s8[16777216]{0:T(1024)(128)(4,1)}), s8[4194304]{0:T(1024)(128)(4,1)S(1)}, s32[]{:S(2)}) async-start(s8[16777216]{0:T(1024)(128)(4,1)} %bitcast.18), calls=%async_computation.1 | async-start | bytes 8388608
  27.0 36.1 %slice-start.2 = ((s8[16777216]{0:T(1024)(128)(4,1)}), s8[4194304]{0:T(1024)(128)(4,1)S(1)}, s32[]{:S(2)}) async-start(s8[16777216]{0:T(1024)(128)(4,1)} %bitcast.18), calls=%async_computation.2 | async-start | bytes 8388608
  55.1 8.1 %slice-start.3 = ((s8[16777216]{0:T(1024)(128)(4,1)}), s8[4194304]{0:T(1024)(128)(4,1)S(1)}, s32[]{:S(2)}) async-start(s8[16777216]{0:T(1024)(128)(4,1)} %bitcast.18), calls=%async_computation.3 | async-start | bytes 8388608
  55.1 8.1 %copy-start.7 = (bf16[8192,128]{1,0:T(8,128)(2,1)S(1)}, bf16[8192,128]{1,0:T(8,128)(2,1)}, u32[]{:S(2)}) copy-start(bf16[8192,128]{1,0:T(8,128)(2,1)} %refs_1_.1) | copy-start | bytes 6291460
  55.1 8.1 %copy-start.10 = (bf16[8192,128]{1,0:T(8,128)(2,1)S(1)}, bf16[8192,128]{1,0:T(8,128)(2,1)}, u32[]{:S(2)}) copy-start(bf16[8192,128]{1,0:T(8,128)(2,1)} %refs_2_.1) | copy-start | bytes 6291460
  55.1 8.1 %copy-start.20 = (f32[1024]{0:T(1024)S(1)}, f32[1024]{0:T(1024)}, u32[]{:S(2)}) copy-start(f32[1024]{0:T(1024)} %param.24) | copy-start | bytes 12292
  58.7 4.4 %collective-permute-start.13 = (bf16[560,2048]{1,0:T(8,128)(2,1)S(1)}, bf16[560,2048]{1,0:T(8,128)(2,1)S(1)}, u32[]{:S(2)}, u32[]{:S(2)}) collective-permute-start(bf16[560,2048]{1,0:T(8,128)(2,1)S(1)} %collective-permute-done.10.refs_2_), channel_id=1, source_target_pairs={{0,1},{1,0},{2,3},{3,2},{4,5},{5,4},{6,7},{7,6},{8,9},{9,8},{10,11... | collective-permute-start | bytes 6881288 | tf_op jit(solution)/shard_map/ppermute | solution.py:27
  58.7 18.4 %collective-permute-start.12 = (bf16[320,2048]{1,0:T(8,128)(2,1)S(1)}, bf16[320,2048]{1,0:T(8,128)(2,1)S(1)}, u32[]{:S(2)}, u32[]{:S(2)}) collective-permute-start(bf16[320,2048]{1,0:T(8,128)(2,1)S(1)} %pack.5.refs_0_), channel_id=1, source_target_pairs={{0,1},{1,0},{2,3},{3,2},{4,5},{5,4},{6,7},{7,6},{8,9},{9,8},{10,11... | collective-permute-start | bytes 3932168 | tf_op jit(solution)/shard_map/ppermute | solution.py:27
  59.2 30.8 %collective-permute-start.11 = (bf16[320,2048]{1,0:T(8,128)(2,1)S(1)}, bf16[320,2048]{1,0:T(8,128)(2,1)}, u32[]{:S(2)}, u32[]{:S(2)}) collective-permute-start(bf16[320,2048]{1,0:T(8,128)(2,1)S(1)} %pack.5.refs_0_), channel_id=1, source_target_pairs={{0,2},{1,3},{2,0},{3,1},{4,6},{5,7},{6,4},{7,5},{8,10},{9,11},{10,... | collective-permute-start | bytes 3932168 | tf_op jit(solution)/shard_map/ppermute | solution.py:27
  61.4 15.7 %copy-start.16 = (f32[160,128]{1,0:T(8,128)}, f32[160,128]{1,0:T(8,128)S(1)}, u32[]{:S(2)}) copy-start(f32[160,128]{1,0:T(8,128)S(1)} %get-tuple-element.276.refs_13_.refs_11_) | copy-start | bytes 245764
  83.8 4.0 %copy-start = (bf16[4096,1280]{1,0:T(8,128)(2,1)}, bf16[4096,1280]{1,0:T(8,128)(2,1)S(1)}, u32[]{:S(2)}) copy-start(bf16[4096,1280]{1,0:T(8,128)(2,1)S(1)} %stage.1.refs_2_.refs_5_) | copy-start | bytes 31457284
  90.0 8.0 %collective-permute-start.14 = (bf16[320,2048]{1,0:T(8,128)(2,1)}, bf16[320,2048]{1,0:T(8,128)(2,1)S(1)}, u32[]{:S(2)}, u32[]{:S(2)}) collective-permute-start(bf16[320,2048]{1,0:T(8,128)(2,1)} %collective-permute-done.11.refs_0_), channel_id=1, source_target_pairs={{0,1},{1,0},{2,3},{3,2},{4,5},{5,4},{6,7},{7,6},{8,9},{9,8},{10,11... | collective-permute-start | bytes 3932168 | tf_op jit(solution)/shard_map/ppermute | solution.py:27
  90.6 4.0 %copy-start.1 = (bf16[4096,1280]{1,0:T(8,128)(2,1)S(1)}, bf16[4096,1280]{1,0:T(8,128)(2,1)}, u32[]{:S(2)}) copy-start(bf16[4096,1280]{1,0:T(8,128)(2,1)} %copy-done) | copy-start | bytes 31457284
  105.1 13.1 %copy-start.22 = (f32[8,160]{1,0:T(8,128)S(1)}, f32[8,160]{1,0:T(8,128)}, u32[]{:S(2)}) copy-start(f32[8,160]{1,0:T(8,128)} %param.17) | copy-start | bytes 15364
  105.1 6.3 %collective-permute-start.15 = (f32[2,160]{1,0:T(2,128)S(1)}, f32[2,160]{1,0:T(2,128)S(1)}, u32[]{:S(2)}, u32[]{:S(2)}) collective-permute-start(f32[2,160]{1,0:T(2,128)S(1)} %get-tuple-element.262), channel_id=1, source_target_pairs={{0,4},{4,0},{8,12},{12,8},{16,20},{20,16},{24,28},{28,24},{1,5},{5... | collective-permute-start | bytes 3848 | tf_op jit(solution)/shard_map/ppermute | solution.py:27
  106.9 4.5 %collective-permute-start.17 = (f32[1,160]{1,0:T(1,128)S(1)}, f32[1,160]{1,0:T(1,128)S(1)}, u32[]{:S(2)}, u32[]{:S(2)}) collective-permute-start(f32[1,160]{1,0:T(1,128)S(1)} %get-tuple-element.264), channel_id=1, source_target_pairs={{0,8},{4,12},{8,0},{12,4},{16,24},{20,28},{24,16},{28,20},{1,9},{5... | collective-permute-start | bytes 1928 | tf_op jit(solution)/shard_map/ppermute | solution.py:27
  108.5 4.5 %collective-permute-start.16 = (f32[1,160]{1,0:T(1,128)S(1)}, f32[1,160]{1,0:T(1,128)S(1)}, u32[]{:S(2)}, u32[]{:S(2)}) collective-permute-start(f32[1,160]{1,0:T(1,128)S(1)} %get-tuple-element.263), channel_id=1, source_target_pairs={{0,16},{4,20},{8,24},{12,28},{16,0},{20,4},{24,8},{28,12},{1,17},{... | collective-permute-start | bytes 1928 | tf_op jit(solution)/shard_map/ppermute | solution.py:27
  113.1 1.2 collective-permute-start.18
  114.3 3.7 %collective-permute-start.19 = (f32[8,160]{1,0:T(8,128)S(1)}, f32[8,160]{1,0:T(8,128)S(1)}, u32[]{:S(2)}, u32[]{:S(2)}) collective-permute-start(f32[8,160]{1,0:T(8,128)S(1)} %fusion.29), channel_id=1, source_target_pairs={{0,2},{1,3},{2,0},{3,1},{4,6},{5,7},{6,4},{7,5},{8,10},{9,11},{10,... | collective-permute-start | bytes 15368 | tf_op jit(solution)/shard_map/ppermute | solution.py:27
  118.1 0.9 copy-start.21
